TPU v7x, 1024 devices: a whole 4x4x32 slice. The times are simulated.
1024 devices in a mesh: lon: 64 (over x_lo, z), hid: 16 (over x_hi, y, core).
Axes of the slice: x: 4 (x_hi: 2, x_lo: 2; x = x_hi * 2 + x_lo), y: 4, z: 32, core: 2. Of those that a mesh axis runs over, the one named last changes fastest.
Arguments:
- observations: bfloat16 [2097152, 64], P('lon'), may hold values from -6 to 6
- block_owner: int32 [16384, 1], P('lon'), may hold values from 0 to 63; in each aligned block of 64 rows (0 to 63, 64 to 127, ...) at most 2 rows name the same one
- block_tile: int32 [16384], P('lon'), may hold values from 0 to 9
- embed_weight: bfloat16 [64, 512], P(None, 'hid'), may hold values from -0.75 to 0.75
- embed_bias: float32 [512], P('hid'), may hold values from -1.5 to 1.5
- mesh_latent: bfloat16 [81920, 512], P('lon', 'hid'), may hold values from -6 to 6
- norm_gain: float32 [512], replicated, may hold values from 0.5 to 1.5
- w_gate: bfloat16 [512, 512], P(None, 'hid'), may hold values from -0.25 to 0.25
- w_up: bfloat16 [512, 512], P(None, 'hid'), may hold values from -0.25 to 0.25
- w_down: bfloat16 [512, 512], P('hid'), may hold values from -0.25 to 0.25
Outputs:
- new_latent: bfloat16 [81920, 512], P('lon', 'hid')
Inputs may be any that keep to these rules, and one draw needn't show every extreme that they name: `block_owner`: blocks of one device come in 4 aligned sub-windows of 64 blocks; within one sub-window at most 2 blocks name the same owner, a bound that some block reaches.
All inputs are finite; a program needn't handle non-finite values.
Results may differ from a plain program's by a relative error of at most 0.0055.
Values may be sent and summed in bfloat16 or wider, within the bound.
A program may use at most 64 MiB of HBM per device.

v0:
```python
import math

import jax
import jax.numpy as jnp
from jax import lax
from jax.sharding import PartitionSpec as P

CAP = 2
SUBW = 4


def with_halo(block, sides, width):
    for axis, dim in sides:
        count = lax.axis_size(axis)
        forward = [(i, i + 1) for i in range(count - 1)]
        forward.append((count - 1, 0))
        backward = [(target, source) for source, target in forward]
        low = lax.ppermute(
            lax.slice_in_dim(block, block.shape[dim] - width, None, axis=dim), axis, forward
        )
        high = lax.ppermute(lax.slice_in_dim(block, 0, width, axis=dim), axis, backward)
        block = jnp.concatenate([low, block, high], axis=dim)
    return block


def local(
    observations,
    block_owner,
    block_tile,
    embed_weight,
    embed_bias,
    mesh_latent,
    norm_gain,
    w_gate,
    w_up,
    w_down,
):
    lon_count = lax.axis_size("lon")
    blocks_dev = block_tile.shape[0]
    block_rows = observations.shape[0] // blocks_dev
    lat_part = embed_weight.shape[1]
    tiles_dev = mesh_latent.shape[0] // block_rows
    sub_blocks = blocks_dev // SUBW
    slot_count = lon_count * CAP
    owners_all = block_owner[:, 0]
    slot_iota = jnp.arange(slot_count, dtype=jnp.int32)
    tile_iota = jnp.arange(tiles_dev, dtype=jnp.int32)
    owner_iota = jnp.arange(lon_count, dtype=jnp.int32)
    tile_sums = jnp.zeros((tiles_dev, block_rows * lat_part), jnp.float32)
    embedded = (
        jnp.dot(observations, embed_weight, preferred_element_type=jnp.float32) + embed_bias
    ).astype(jnp.bfloat16)
    outgoing_rows = embedded.reshape(blocks_dev, block_rows * lat_part)
    for window in range(SUBW):
        first_block = window * sub_blocks
        owner_ids = owners_all[first_block : first_block + sub_blocks]
        tile_ids = block_tile[first_block : first_block + sub_blocks]
        owner_hits = (owner_ids[:, None] == owner_iota[None, :]).astype(jnp.int32)
        earlier = jnp.cumsum(owner_hits, axis=0) - owner_hits
        slot_rank = jnp.sum(earlier * owner_hits, axis=1)
        slot_of = owner_ids * CAP + slot_rank
        placed = slot_iota[:, None] == slot_of[None, :]
        send_tiles = jnp.sum(jnp.where(placed, tile_ids[None, :] + 1, 0), axis=1) - 1
        placer = placed.astype(jnp.bfloat16)
        outgoing = jnp.dot(
            placer,
            outgoing_rows[first_block : first_block + sub_blocks],
            preferred_element_type=jnp.float32,
        ).astype(jnp.bfloat16)
        arrived, arrived_tiles = (
            lax.all_to_all(outgoing, "lon", split_axis=0, concat_axis=0, tiled=True),
            lax.all_to_all(send_tiles, "lon", split_axis=0, concat_axis=0, tiled=True),
        )
        tile_hits = (arrived_tiles[None, :] == tile_iota[:, None]).astype(jnp.bfloat16)
        tile_sums = tile_sums + jnp.dot(tile_hits, arrived, preferred_element_type=jnp.float32)
    padded = with_halo(tile_sums, (("lon", 0),), 1)
    smooth = padded[1:-1] + 0.5 * (padded[:-2] + padded[2:])
    agg_scale = math.sqrt(tiles_dev / blocks_dev)
    node_rows = tiles_dev * block_rows
    latent_f = mesh_latent.astype(jnp.float32)
    mixed_latent = (latent_f + agg_scale * smooth.reshape(node_rows, lat_part)).astype(jnp.bfloat16)
    whole_latent = lax.all_gather(mixed_latent, "hid", axis=1, tiled=True).astype(jnp.float32)
    mean_square = jnp.mean(whole_latent * whole_latent, axis=1, keepdims=True)
    normed = (whole_latent * lax.rsqrt(mean_square + 1e-05) * norm_gain).astype(jnp.bfloat16)
    gate_proj = jnp.dot(normed, w_gate, preferred_element_type=jnp.float32)
    up_proj = jnp.dot(normed, w_up, preferred_element_type=jnp.float32)
    hidden = (jax.nn.silu(gate_proj) * up_proj).astype(jnp.bfloat16)
    partial_value = jnp.dot(hidden, w_down, preferred_element_type=jnp.float32)
    summed = lax.psum_scatter(partial_value, "hid", scatter_dimension=1, tiled=True)
    return (latent_f + summed).astype(jnp.bfloat16)


def solution(mesh):
    return jax.shard_map(
        local,
        mesh=mesh,
        in_specs=(
            P("lon", None),
            P("lon", None),
            P("lon"),
            P(None, "hid"),
            P("hid"),
            P("lon", "hid"),
            P(),
            P(None, "hid"),
            P(None, "hid"),
            P("hid", None),
        ),
        out_specs=P("lon", "hid"),
        check_vma=False,
    )
```

profile of v0, /device:TPU:1, one launch (start us, length us, event | category | flops | bytes accessed | tf_op | source)
XLA Modules:
  0.0 815.9 jit_solution(18002711788036214039)
XLA Ops:
  11.0 30.8 %all-to-all-start = ((s32[64,2,1]{1,2,0:T(1,128)}), s32[64,2,1]{1,2,0:T(1,128)S(1)}, u32[]{:S(2)}, u32[]{:S(2)}) async-start(s32[64,2,1]{1,2,0:T(1,128)} %bitcast.1), calls=%async_computation | async-start | bytes 65536 | tf_op jit(solution)/shard_map/all_to_all | solution.py:72
  41.8 2.9 fusion
  46.8 17.1 %all-to-all-done = s32[64,2,1]{1,2,0:T(1,128)S(1)} async-done(((s32[64,2,1]{1,2,0:T(1,128)}), s32[64,2,1]{1,2,0:T(1,128)S(1)}, u32[]{:S(2)}, u32[]{:S(2)}) %all-to-all-start) | async-done | bytes 544 | tf_op jit(solution)/shard_map/all_to_all | solution.py:72
  64.0 5.6 all-to-all-start.2
  70.4 21.3 %all-to-all-done.2 = s32[64,2,1]{1,2,0:T(1,128)S(1)} async-done(((s32[64,2,1]{1,2,0:T(1,128)}), s32[64,2,1]{1,2,0:T(1,128)S(1)}, u32[]{:S(2)}, u32[]{:S(2)}) %all-to-all-start.2) | async-done | bytes 544 | tf_op jit(solution)/shard_map/all_to_all | solution.py:72
  91.7 4.6 all-to-all-start.4
  100.4 18.0 %all-to-all-done.4 = s32[64,2,1]{1,2,0:T(1,128)S(1)} async-done(((s32[64,2,1]{1,2,0:T(1,128)}), s32[64,2,1]{1,2,0:T(1,128)S(1)}, u32[]{:S(2)}, u32[]{:S(2)}) %all-to-all-start.4) | async-done | bytes 544 | tf_op jit(solution)/shard_map/all_to_all | solution.py:72
  118.5 4.7 all-to-all-start.6
  125.2 20.1 %all-to-all-done.6 = s32[64,2,1]{1,2,0:T(1,128)S(1)} async-done(((s32[64,2,1]{1,2,0:T(1,128)}), s32[64,2,1]{1,2,0:T(1,128)S(1)}, u32[]{:S(2)}, u32[]{:S(2)}) %all-to-all-start.6) | async-done | bytes 544 | tf_op jit(solution)/shard_map/all_to_all | solution.py:72
  145.3 4.7 all-to-all-start.1
  151.9 3.0 slice.83
  158.0 79.7 %all-to-all-done.1 = bf16[64,2,4096]{2,1,0:T(2,128)(2,1)S(1)} async-done(((bf16[64,2,4096]{2,1,0:T(2,128)(2,1)}), bf16[64,2,4096]{2,1,0:T(2,128)(2,1)S(1)}, u32[]{:S(2)}, u32[]{:S(2)}) %all-to-all-start.1) | async-done | bytes 1048608 | tf_op jit(solution)/shard_map/all_to_all | solution.py:71
  237.7 25.0 %all-to-all-start.3 = ((bf16[64,2,4096]{2,1,0:T(2,128)(2,1)}), bf16[64,2,4096]{2,1,0:T(2,128)(2,1)}, u32[]{:S(2)}, u32[]{:S(2)}) async-start(bf16[64,2,4096]{2,1,0:T(2,128)(2,1)} %all_to_all.53), calls=%async_computation.3 | async-start | bytes 2097152 | tf_op jit(solution)/shard_map/all_to_all | solution.py:71
  264.6 3.0 slice.88
  270.7 81.2 %all-to-all-done.3 = bf16[64,2,4096]{2,1,0:T(2,128)(2,1)} async-done(((bf16[64,2,4096]{2,1,0:T(2,128)(2,1)}), bf16[64,2,4096]{2,1,0:T(2,128)(2,1)}, u32[]{:S(2)}, u32[]{:S(2)}) %all-to-all-start.3) | async-done | bytes 1048608 | tf_op jit(solution)/shard_map/all_to_all | solution.py:71
  351.8 24.7 %all-to-all-start.5 = ((bf16[64,2,4096]{2,1,0:T(2,128)(2,1)}), bf16[64,2,4096]{2,1,0:T(2,128)(2,1)}, u32[]{:S(2)}, u32[]{:S(2)}) async-start(bf16[64,2,4096]{2,1,0:T(2,128)(2,1)} %all_to_all.57), calls=%async_computation.5 | async-start | bytes 2097152 | tf_op jit(solution)/shard_map/all_to_all | solution.py:71
  378.5 3.0 slice.93
  384.6 82.3 %all-to-all-done.5 = bf16[64,2,4096]{2,1,0:T(2,128)(2,1)} async-done(((bf16[64,2,4096]{2,1,0:T(2,128)(2,1)}), bf16[64,2,4096]{2,1,0:T(2,128)(2,1)}, u32[]{:S(2)}, u32[]{:S(2)}) %all-to-all-start.5) | async-done | bytes 1048608 | tf_op jit(solution)/shard_map/all_to_all | solution.py:71
  466.9 23.3 %all-to-all-start.7 = ((bf16[64,2,4096]{2,1,0:T(2,128)(2,1)}), bf16[64,2,4096]{2,1,0:T(2,128)(2,1)S(1)}, u32[]{:S(2)}, u32[]{:S(2)}) async-start(bf16[64,2,4096]{2,1,0:T(2,128)(2,1)} %all_to_all.61), calls=%async_computation.7 | async-start | bytes 2097152 | tf_op jit(solution)/shard_map/all_to_all | solution.py:71
  500.4 80.2 %all-to-all-done.7 = bf16[64,2,4096]{2,1,0:T(2,128)(2,1)S(1)} async-done(((bf16[64,2,4096]{2,1,0:T(2,128)(2,1)}), bf16[64,2,4096]{2,1,0:T(2,128)(2,1)S(1)}, u32[]{:S(2)}, u32[]{:S(2)}) %all-to-all-start.7) | async-done | bytes 1048608 | tf_op jit(solution)/shard_map/all_to_all | solution.py:71
  581.3 4.3 collective-permute-start.1
  587.8 4.6 collective-permute-done
  593.6 83.3 %all-gather.2.cloned.1.call-done = bf16[1280,512]{0,1:T(8,128)(2,1)} async-done(((bf16[1280,32]{0,1:T(8,128)(2,1)}), bf16[1280,512]{0,1:T(8,128)(2,1)}) %all-gather.2.cloned.1.call-update) | async-done | bytes 1310736 | tf_op jit(solution)/shard_map/all_gather | solution.py:82
  682.9 124.7 %reduce-scatter.2.cloned.1.call-done = f32[1280,32]{0,1:T(8,128)} async-done(((f32[1280,512]{0,1:T(8,128)}), f32[1280,32]{0,1:T(8,128)}) %reduce-scatter.2.cloned.1.call-update) | async-done | bytes 163856 | tf_op jit(solution)/shard_map/reduce_scatter | solution.py:89
  (84 shorter events, 50.3 us)
Async XLA Ops:
  6.5 673.9 %copy-start = (bf16[32,512]{1,0:T(8,128)(2,1)S(1)}, bf16[32,512]{1,0:T(8,128)(2,1)}, u32[]{:S(2)}) copy-start(bf16[32,512]{1,0:T(8,128)(2,1)} %param.19) | copy-start | bytes 98308
  11.0 53.0 %all-to-all-start = ((s32[64,2,1]{1,2,0:T(1,128)}), s32[64,2,1]{1,2,0:T(1,128)S(1)}, u32[]{:S(2)}, u32[]{:S(2)}) async-start(s32[64,2,1]{1,2,0:T(1,128)} %bitcast.1), calls=%async_computation | async-start | bytes 65536 | tf_op jit(solution)/shard_map/all_to_all | solution.py:72
  64.0 27.8 %all-to-all-start.2 = ((s32[64,2,1]{1,2,0:T(1,128)}), s32[64,2,1]{1,2,0:T(1,128)S(1)}, u32[]{:S(2)}, u32[]{:S(2)}) async-start(s32[64,2,1]{1,2,0:T(1,128)} %bitcast.3), calls=%async_computation.2 | async-start | bytes 65536 | tf_op jit(solution)/shard_map/all_to_all | solution.py:72
  91.7 26.7 %all-to-all-start.4 = ((s32[64,2,1]{1,2,0:T(1,128)}), s32[64,2,1]{1,2,0:T(1,128)S(1)}, u32[]{:S(2)}, u32[]{:S(2)}) async-start(s32[64,2,1]{1,2,0:T(1,128)} %bitcast.5), calls=%async_computation.4 | async-start | bytes 65536 | tf_op jit(solution)/shard_map/all_to_all | solution.py:72
  118.5 26.9 %all-to-all-start.6 = ((s32[64,2,1]{1,2,0:T(1,128)}), s32[64,2,1]{1,2,0:T(1,128)S(1)}, u32[]{:S(2)}, u32[]{:S(2)}) async-start(s32[64,2,1]{1,2,0:T(1,128)} %bitcast.7), calls=%async_computation.6 | async-start | bytes 65536 | tf_op jit(solution)/shard_map/all_to_all | solution.py:72
  145.3 92.4 %all-to-all-start.1 = ((bf16[64,2,4096]{2,1,0:T(2,128)(2,1)}), bf16[64,2,4096]{2,1,0:T(2,128)(2,1)S(1)}, u32[]{:S(2)}, u32[]{:S(2)}) async-start(bf16[64,2,4096]{2,1,0:T(2,128)(2,1)} %all_to_all.49), calls=%async_computation.1 | async-start | bytes 2097152 | tf_op jit(solution)/shard_map/all_to_all | solution.py:71
  237.7 114.1 %all-to-all-start.3 = ((bf16[64,2,4096]{2,1,0:T(2,128)(2,1)}), bf16[64,2,4096]{2,1,0:T(2,128)(2,1)}, u32[]{:S(2)}, u32[]{:S(2)}) async-start(bf16[64,2,4096]{2,1,0:T(2,128)(2,1)} %all_to_all.53), calls=%async_computation.3 | async-start | bytes 2097152 | tf_op jit(solution)/shard_map/all_to_all | solution.py:71
  351.8 115.1 %all-to-all-start.5 = ((bf16[64,2,4096]{2,1,0:T(2,128)(2,1)}), bf16[64,2,4096]{2,1,0:T(2,128)(2,1)}, u32[]{:S(2)}, u32[]{:S(2)}) async-start(bf16[64,2,4096]{2,1,0:T(2,128)(2,1)} %all_to_all.57), calls=%async_computation.5 | async-start | bytes 2097152 | tf_op jit(solution)/shard_map/all_to_all | solution.py:71
  466.9 113.7 %all-to-all-start.7 = ((bf16[64,2,4096]{2,1,0:T(2,128)(2,1)}), bf16[64,2,4096]{2,1,0:T(2,128)(2,1)S(1)}, u32[]{:S(2)}, u32[]{:S(2)}) async-start(bf16[64,2,4096]{2,1,0:T(2,128)(2,1)} %all_to_all.61), calls=%async_computation.7 | async-start | bytes 2097152 | tf_op jit(solution)/shard_map/all_to_all | solution.py:71
  490.2 186.7 %all-gather.2.cloned.1.call-start = ((), (), s32[]{:S(2)}) async-start(), calls=%async_computation.9 | async-start | bytes 1392640 | tf_op jit(solution)/shard_map/all_gather | solution.py:82
  581.0 11.8 %copy-start.2 = (bf16[1280,32]{0,1:T(8,128)(2,1)S(1)}, bf16[1280,32]{0,1:T(8,128)(2,1)}, u32[]{:S(2)}) copy-start(bf16[1280,32]{0,1:T(8,128)(2,1)} %param.15) | copy-start | bytes 245764
  581.3 97.4 %copy-start.4 = (f32[512]{0:T(512)S(1)}, f32[512]{0:T(512)}, u32[]{:S(2)}) copy-start(f32[512]{0:T(512)} %param.16) | copy-start | bytes 6148
  581.3 97.4 %copy-start.5 = (bf16[512,32]{0,1:T(8,128)(2,1)S(1)}, bf16[512,32]{0,1:T(8,128)(2,1)}, u32[]{:S(2)}) copy-start(bf16[512,32]{0,1:T(8,128)(2,1)} %param.17) | copy-start | bytes 98308
  581.3 6.4 collective-permute-start.1
  585.6 6.7 collective-permute-start
  592.9 87.6 %copy-start.3 = (bf16[512,32]{0,1:T(8,128)(2,1)S(1)}, bf16[512,32]{0,1:T(8,128)(2,1)}, u32[]{:S(2)}) copy-start(bf16[512,32]{0,1:T(8,128)(2,1)} %param.18) | copy-start | bytes 98308
  593.5 214.0 %reduce-scatter.2.cloned.1.call-start = ((), (), s32[]{:S(2)}) async-start(), calls=%async_computation.10 | async-start | bytes 2785280 | tf_op jit(solution)/shard_map/reduce_scatter | solution.py:89
  676.9 3.6 copy-start.1
Sparse Core Ops, SparseCore 0:
  593.7 83.2 all-gather.1
  683.0 124.4 reduce-scatter.1
where the time goes:
time: 817 us; the launch traced here: 816 us
  waiting for transfers between devices  612 us (75%)
  starting transfers between devices  130 us (16%)
  local copies, waits for them, and re-layouts  35.2 us (4%)
  matrix products  14.6 us (2%)
  between operations  13.8 us (2%)
  other arithmetic  10.1 us (1%)
    all_to_all x4, waiting for transfers between devices, local(): lax.all_to_all(outgoing, 'lon', split_axis=0, concat_axis=0, tiled=True)  323 us
    reduce_scatter x1, waiting for transfers between devices, local(): lax.psum_scatter(partial_value, 'hid', scatter_dimension=1, tiled=True)  125 us
    all_gather x1, waiting for transfers between devices, local(): lax.all_gather(mixed_latent, 'hid', axis=1, tiled=True).astype(jnp.float32)  83.3 us
    all_to_all x4, starting transfers between devices, local(): lax.all_to_all(outgoing, 'lon', split_axis=0, concat_axis=0, tiled=True)  77.6 us
    all_to_all x4, waiting for transfers between devices, local(): lax.all_to_all(send_tiles, 'lon', split_axis=0, concat_axis=0, tiled=True)  76.6 us
    all_to_all x4, starting transfers between devices, local(): lax.all_to_all(send_tiles, 'lon', split_axis=0, concat_axis=0, tiled=True)  45.7 us
    slice x9, local copies, waits for them, and re-layouts, local(): outgoing_rows[first_block:first_block + sub_blocks]  19.2 us
  transfers between devices with their start and end apart: 12, of which 11 were waited for; matrix products, arithmetic and copies ran while one was open for 4% of the time, Pallas kernels for 0%

commit v1 on v0

v1 whole, which is shorter than its diff:
```python
import math

import jax
import jax.numpy as jnp
from jax import lax
from jax.sharding import PartitionSpec as P

BLK = 128
PAD = 16


def local(
    observations,
    block_owner,
    block_tile,
    embed_weight,
    embed_bias,
    mesh_latent,
    norm_gain,
    w_gate,
    w_up,
    w_down,
):
    lon = lax.axis_size("lon")
    hid = lax.axis_size("hid")
    h = lax.axis_index("hid")
    blocks = block_tile.shape[0]
    channels = observations.shape[1]
    tiles_dev = mesh_latent.shape[0] // BLK
    tiles = tiles_dev * lon
    part = channels // hid
    wg = lax.all_gather(w_gate, "hid", axis=1, tiled=True)
    wu = lax.all_gather(w_up, "hid", axis=1, tiled=True)
    wd = lax.all_gather(w_down, "hid", axis=0, tiled=True)
    we = lax.all_gather(embed_weight, "hid", axis=1, tiled=True)
    bias = lax.all_gather(embed_bias, "hid", axis=0, tiled=True)
    latent = lax.all_to_all(mesh_latent, "hid", split_axis=0, concat_axis=1, tiled=True)

    mine = lax.dynamic_slice_in_dim(observations.T, h * part, part, axis=0)
    data = mine.reshape(part, blocks, BLK).transpose(1, 0, 2).reshape(blocks, part * BLK)
    target = block_owner[:, 0] * tiles_dev + block_tile
    gap = lax.rem(jnp.arange(tiles, dtype=jnp.int32)[:, None] - target[None, :] + tiles, tiles)
    spread = jnp.where(gap == 0, 1.0, jnp.where((gap == 1) | (gap == tiles - 1), 0.5, 0.0))
    sums = jnp.dot(spread.astype(jnp.bfloat16), data, preferred_element_type=jnp.float32)
    counts = jnp.sum(spread, axis=1).reshape(lon, 1, tiles_dev)
    counts = jnp.pad(counts, ((0, 0), (0, PAD - 1 - tiles_dev), (0, part * BLK - tiles_dev)))
    sums = jnp.concatenate([sums.reshape(lon, tiles_dev, part * BLK), counts], axis=1)
    sums = lax.psum_scatter(sums.reshape(lon * PAD, part * BLK), "lon", scatter_dimension=0, tiled=True)
    n_tile = sums[tiles_dev, :tiles_dev]
    nodes = sums[:tiles_dev].reshape(tiles_dev, part, BLK).transpose(1, 0, 2).reshape(part, tiles_dev * BLK)
    nodes = lax.all_to_all(nodes, "hid", split_axis=1, concat_axis=0, tiled=True)
    share = nodes.shape[1]
    n_node = lax.dynamic_slice_in_dim(jnp.repeat(n_tile, BLK), h * share, share, axis=0)
    smooth = jnp.dot(nodes.T, we.astype(jnp.float32), precision=lax.Precision.HIGHEST) + n_node[:, None] * bias
    latent_f = latent.astype(jnp.float32)
    mixed = (latent_f + math.sqrt(tiles_dev / blocks) * smooth).astype(jnp.bfloat16).astype(jnp.float32)
    mean_square = jnp.mean(mixed * mixed, axis=1, keepdims=True)
    normed = (mixed * lax.rsqrt(mean_square + 1e-05) * norm_gain).astype(jnp.bfloat16)
    gate = jnp.dot(normed, wg, preferred_element_type=jnp.float32)
    up = jnp.dot(normed, wu, preferred_element_type=jnp.float32)
    hidden = (jax.nn.silu(gate) * up).astype(jnp.bfloat16)
    out = (latent_f + jnp.dot(hidden, wd, preferred_element_type=jnp.float32)).astype(jnp.bfloat16)
    return lax.all_to_all(out, "hid", split_axis=1, concat_axis=0, tiled=True)


def solution(mesh):
    return jax.shard_map(
        local,
        mesh=mesh,
        in_specs=(
            P("lon", None),
            P("lon", None),
            P("lon"),
            P(None, "hid"),
            P("hid"),
            P("lon", "hid"),
            P(),
            P(None, "hid"),
            P(None, "hid"),
            P("hid", None),
        ),
        out_specs=P("lon", "hid"),
        check_vma=False,
    )
```

time: 817 us -> 325 us (0.40)
  waiting for transfers between devices: 612 us -> 90.8 us
  blocking collectives: 0 us -> 132 us
  starting transfers between devices: 130 us -> 73.1 us
  local copies, waits for them, and re-layouts: 35.2 us -> 10.6 us
  matrix products: 14.6 us -> 1.73 us
    all_to_all x8 -> x2, waiting for transfers between devices: 400 us -> 6.48 us  [the longest x1 6.48 us: local(): lax.all_to_all(nodes, 'hid', split_axis=1, concat_axis=0, tiled=True)]
    all_gather x0 -> x4, blocking collectives: none -> 89 us  [the longest x1 25.9 us: local(): wg = lax.all_gather(w_gate, 'hid', axis=1, tiled=True)]
    all_gather x1 -> x0, waiting for transfers between devices: 83.3 us -> none  [local(): lax.all_gather(mixed_latent, 'hid', axis=1, tiled=True).astype(jnp.float32)]
    all_to_all x8 -> x2, starting transfers between devices: 123 us -> 73.1 us  [the longest x1 55.6 us: local(): lax.all_to_all(nodes, 'hid', split_axis=1, concat_axis=0, tiled=True)]
    reduce_scatter x1, waiting for transfers between devices: 125 us -> 84.3 us  [local(): lax.psum_scatter(sums.reshape(lon * PAD, part * BLK), 'lon', scatter_dime...]
    unnamed x0 -> x1, blocking collectives: none -> 32.7 us
    slice x11 -> x0, local copies, waits for them, and re-layouts: 20.1 us -> none  [the longest x9 19.2 us: local(): outgoing_rows[first_block:first_block + sub_blocks]]
    dot_general x11 -> x4, matrix products: 14.6 us -> 1.73 us  [the longest x1 0.57 us: local(): jnp.dot(spread.astype(jnp.bfloat16), data, preferred_element_type=jnp.flo...]
  transfers between devices with their start and end apart: 12 -> 3, of which waited for: 11 -> 2; matrix products, arithmetic and copies ran while one was open for 4% -> 1% of each run, Pallas kernels for 0% -> 0%
where the time goes in v1:
time: 325 us
  blocking collectives  132 us (41%)
  waiting for transfers between devices  90.8 us (28%)
  starting transfers between devices  73.1 us (22%)
  between operations  14.2 us (4%)
  local copies, waits for them, and re-layouts  10.6 us (3%)
    reduce_scatter x1, waiting for transfers between devices, local(): lax.psum_scatter(sums.reshape(lon * PAD, part * BLK), 'lon', scatter_dime...  84.3 us
    all_to_all x1, starting transfers between devices, local(): lax.all_to_all(nodes, 'hid', split_axis=1, concat_axis=0, tiled=True)  55.6 us
    unnamed x1, blocking collectives  32.7 us
    all_gather x1, blocking collectives, local(): wg = lax.all_gather(w_gate, 'hid', axis=1, tiled=True)  25.9 us
    all_gather x1, blocking collectives, local(): wd = lax.all_gather(w_down, 'hid', axis=0, tiled=True)  22.1 us
    all_gather x1, blocking collectives, local(): wu = lax.all_gather(w_up, 'hid', axis=1, tiled=True)  20.9 us
    all_gather x1, blocking collectives, local(): we = lax.all_gather(embed_weight, 'hid', axis=1, tiled=True)  20.2 us
    all_to_all x1, starting transfers between devices, local(): lax.all_to_all(mesh_latent, 'hid', split_axis=0, concat_axis=1, tiled=True)  17.5 us
  transfers between devices with their start and end apart: 3, of which 2 were waited for; matrix products, arithmetic and copies ran while one was open for 1% of the time, Pallas kernels for 0%

profile of v1, /device:TPU:1, one launch (start us, length us, event | category | flops | bytes accessed | tf_op | source)
XLA Modules:
  0.0 324.8 jit_solution(13825768980888415618)
XLA Ops:
  6.5 1.2 dynamic-slice_bitcast_fusion
  7.8 0.7 broadcast_multiply_fusion
  8.5 0.7 add.51
  9.2 0.5 select_reduce_fusion
  9.8 0.6 fusion.14
  10.7 2.6 copy.42
  13.3 0.8 copy-done
  14.3 0.7 copy.40
  15.0 17.5 %all-to-all-start = ((bf16[16,80,32]{1,2,0:T(8,128)(2,1)}), bf16[16,80,32]{1,2,0:T(8,128)(2,1)S(1)}, u32[]{:S(2)}, u32[]{:S(2)}) async-start(bf16[16,80,32]{1,2,0:T(8,128)(2,1)} %copy.40), calls=%async_computation | async-start | bytes 262144 | tf_op jit(solution)/shard_map/all_to_all | solution.py:37
  32.4 25.9 %all_gather.17 = bf16[512,512]{0,1:T(8,128)(2,1)S(1)} all-gather(bf16[512,32]{0,1:T(8,128)(2,1)S(1)} %copy-done.1), channel_id=1, replica_groups=mesh['lon'=64,'hid'=16] {'hid'}, dimensions={1}, use_global_device_ids=true | all-gather | bytes 557056 | tf_op jit(solution)/shard_map/all_gather | solution.py:32
  58.4 20.9 %all_gather.18 = bf16[512,512]{0,1:T(8,128)(2,1)S(1)} all-gather(bf16[512,32]{0,1:T(8,128)(2,1)S(1)} %copy-done.2), channel_id=1, replica_groups=mesh['lon'=64,'hid'=16] {'hid'}, dimensions={1}, use_global_device_ids=true | all-gather | bytes 557056 | tf_op jit(solution)/shard_map/all_gather | solution.py:33
  79.2 22.1 %all_gather.19 = bf16[512,512]{1,0:T(8,128)(2,1)S(1)} all-gather(bf16[32,512]{1,0:T(8,128)(2,1)S(1)} %copy-done.3), channel_id=1, replica_groups=mesh['lon'=64,'hid'=16] {'hid'}, dimensions={0}, use_global_device_ids=true | all-gather | bytes 557056 | tf_op jit(solution)/shard_map/all_gather | solution.py:34
  101.3 1.3 dynamic-slice.4
  103.5 32.7 %all-reduce.1 = f32[512]{0:T(512)S(1)} all-reduce(f32[512]{0:T(512)S(1)} %dynamic-update-slice), channel_id=1, replica_groups=mesh['lon'=64,'hid'=16] {'hid'}, use_global_device_ids=true, to_apply=%add.1 | all-reduce | flops 512 | bytes 4096
  136.2 20.2 %all_gather.15 = bf16[64,512]{0,1:T(8,128)(2,1)S(1)} all-gather(bf16[64,32]{0,1:T(8,128)(2,1)S(1)} %copy-done.4), channel_id=1, replica_groups=mesh['lon'=64,'hid'=16] {'hid'}, dimensions={1}, use_global_device_ids=true | all-gather | bytes 69632 | tf_op jit(solution)/shard_map/all_gather | solution.py:35
  156.5 84.3 %reduce-scatter.2.cloned.1.call-done = f32[16,512]{1,0:T(8,128)} async-done(((f32[1024,512]{1,0:T(8,128)}), f32[16,512]{1,0:T(8,128)}) %reduce-scatter.2.cloned.1.call-update) | async-done | bytes 32784 | tf_op jit(solution)/shard_map/reduce_scatter | solution.py:48
  240.8 0.8 reshape.77
  241.7 0.6 copy.44
  242.3 55.6 %all-to-all-start.1 = ((f32[4,16,80]{2,0,1:T(4,128)}), f32[4,16,80]{2,0,1:T(4,128)S(1)}, u32[]{:S(2)}, u32[]{:S(2)}) async-start(f32[4,16,80]{2,0,1:T(4,128)} %copy.44), calls=%async_computation.2 | async-start | bytes 65536 | tf_op jit(solution)/shard_map/all_to_all | solution.py:51
  298.0 0.7 slice_bitcast_fusion
  298.8 6.5 %all-to-all-done.1 = f32[4,16,80]{2,0,1:T(4,128)S(1)} async-done(((f32[4,16,80]{2,0,1:T(4,128)}), f32[4,16,80]{2,0,1:T(4,128)S(1)}, u32[]{:S(2)}, u32[]{:S(2)}) %all-to-all-start.1) | async-done | bytes 20512 | tf_op jit(solution)/shard_map/all_to_all | solution.py:51
  306.0 0.5 fusion.5
  306.6 10.5 %all_to_all.51 = bf16[80,16,32]{0,2,1:T(8,128)(2,1)S(1)} all-to-all(bf16[80,16,32]{0,2,1:T(8,128)(2,1)S(1)} %bitcast.37), channel_id=1, replica_groups=mesh['lon'=64,'hid'=16] {'hid'}, dimensions={1} | all-to-all | bytes 163840 | tf_op jit(solution)/shard_map/all_to_all | solution.py:63
  317.2 0.8 all_to_all.47
  (34 shorter events, 2.2 us)
Async XLA Ops:
  6.5 234.3 %reduce-scatter.2.cloned.1.call-start = ((), (), s32[]{:S(2)}) async-start(), calls=%async_computation.4 | async-start | bytes 2129920 | tf_op jit(solution)/shard_map/reduce_scatter | solution.py:48
  13.2 0.9 copy-start
  13.2 19.2 %copy-start.1 = (bf16[512,32]{0,1:T(8,128)(2,1)S(1)}, bf16[512,32]{0,1:T(8,128)(2,1)}, u32[]{:S(2)}) copy-start(bf16[512,32]{0,1:T(8,128)(2,1)} %param.17) | copy-start | bytes 98308
  13.2 45.1 %copy-start.2 = (bf16[512,32]{0,1:T(8,128)(2,1)S(1)}, bf16[512,32]{0,1:T(8,128)(2,1)}, u32[]{:S(2)}) copy-start(bf16[512,32]{0,1:T(8,128)(2,1)} %param.18) | copy-start | bytes 98308
  13.2 66.0 %copy-start.3 = (bf16[32,512]{1,0:T(8,128)(2,1)S(1)}, bf16[32,512]{1,0:T(8,128)(2,1)}, u32[]{:S(2)}) copy-start(bf16[32,512]{1,0:T(8,128)(2,1)} %param.19) | copy-start | bytes 98308
  13.2 90.0 %copy-start.6 = (f32[32]{0:T(128)S(1)}, f32[32]{0:T(128)}, u32[]{:S(2)}) copy-start(f32[32]{0:T(128)} %param.14) | copy-start | bytes 388
  13.2 123.0 %copy-start.4 = (bf16[64,32]{0,1:T(8,128)(2,1)S(1)}, bf16[64,32]{0,1:T(8,128)(2,1)}, u32[]{:S(2)}) copy-start(bf16[64,32]{0,1:T(8,128)(2,1)} %param.13) | copy-start | bytes 12292
  14.1 291.6 %copy-start.5 = (f32[512]{0:T(512)S(1)}, f32[512]{0:T(512)}, u32[]{:S(2)}) copy-start(f32[512]{0:T(512)} %param.16) | copy-start | bytes 6148
  15.0 141.4 %all-to-all-start = ((bf16[16,80,32]{1,2,0:T(8,128)(2,1)}), bf16[16,80,32]{1,2,0:T(8,128)(2,1)S(1)}, u32[]{:S(2)}, u32[]{:S(2)}) async-start(bf16[16,80,32]{1,2,0:T(8,128)(2,1)} %copy.40), calls=%async_computation | async-start | bytes 262144 | tf_op jit(solution)/shard_map/all_to_all | solution.py:37
  242.3 63.0 %all-to-all-start.1 = ((f32[4,16,80]{2,0,1:T(4,128)}), f32[4,16,80]{2,0,1:T(4,128)S(1)}, u32[]{:S(2)}, u32[]{:S(2)}) async-start(f32[4,16,80]{2,0,1:T(4,128)} %copy.44), calls=%async_computation.2 | async-start | bytes 65536 | tf_op jit(solution)/shard_map/all_to_all | solution.py:51
Sparse Core Ops, SparseCore 0:
  13.4 227.3 reduce-scatter.1

commit v2 on v1

v2 whole, which is shorter than its diff:
```python
import functools
import math

import jax
import jax.numpy as jnp
from jax import lax
from jax.experimental import pallas as pl
from jax.experimental.pallas import tpu as pltpu
from jax.sharding import PartitionSpec as P

MESH = pl.DeviceIdType.MESH
BLK = 128
NX = 2
NZ = 32
NH = 16
LON = NX * NZ
QA = 4
KB = NZ // QA
TILES = 10
ROWS = 16
PART = 4
WIDE = 3 * BLK
PIECE = KB * ROWS
F32 = jnp.float32
BF16 = jnp.bfloat16


def kernel(
    scale,
    obs, owner, tile, weight, latent, gain, w_gate, w_up, w_down,
    out,
    slab, rows32, data, part, xin, mine, ain, summed, bin_, tiles_out, tiles_in, w_all, we_all, lat_all, gain_t, out_all,
    load_sem, own_sem, xs, xr, as_, ar, bs, br, ws, wr, es, er, ls, lr, ts, tr, os_, or_,
):
    lon = lax.axis_index("lon")
    h = lax.axis_index("hid")
    x = lon // NZ
    z = lax.rem(lon, NZ)
    off = 2 * lax.rem(h, 2)
    v = lax.rem(z + off, NZ)
    g = v // QA
    q = lax.rem(v, QA)

    def at_v(value):
        return (x * NZ + lax.rem(value - off + NZ, NZ), h)

    x_peer = (lax.rem(x + 1, NX) * NZ + z, h)
    a_peer = [at_v(g * QA + lax.rem(q + d, QA)) for d in range(QA)]
    b_peer = [at_v(lax.rem(g + d, KB) * QA + q) for d in range(KB)]
    h_index = [lax.rem(h + d, NH) for d in range(NH)]
    h_peer = [(lon, i) for i in h_index]

    barrier = pltpu.get_barrier_semaphore()
    peers = [x_peer] + a_peer[1:] + b_peer[1:] + h_peer[1:]
    for peer in peers:
        pl.semaphore_signal(barrier, inc=1, device_id=peer, device_id_type=MESH)

    load = pltpu.make_async_copy(obs.at[pl.ds(pl.multiple_of((h // 4) * 16, 16), 16)], slab, load_sem)
    load.start()
    share = w_down.shape[0]
    own = [
        pltpu.make_async_copy(w_gate, w_all.at[h, 0], own_sem.at[0]),
        pltpu.make_async_copy(w_up, w_all.at[h, 1], own_sem.at[1]),
        pltpu.make_async_copy(w_down, w_all.at[h, 2], own_sem.at[2]),
        pltpu.make_async_copy(weight, we_all.at[h], own_sem.at[3]),
    ]
    for copy in own:
        copy.start()
    gain_t[...] = jnp.broadcast_to(gain[...], (BLK, gain.shape[1])).T

    codes = []
    for step, weigh in ((0, 1.0), (-1, 0.5), (1, 0.5)):
        t = tile[...] + step
        o = owner[...]
        o = jnp.where(t < 0, (o + LON - 1) & (LON - 1), jnp.where(t >= TILES, (o + 1) & (LON - 1), o))
        t = jnp.where(t < 0, TILES - 1, jnp.where(t >= TILES, 0, t))
        u = ((o & (NZ - 1)) + off) & (NZ - 1)
        row = ((o >> 5) * NZ + (u & (QA - 1)) * KB + (u >> 2)) * ROWS + t
        codes.append((weigh, row, jnp.where(t < 6, row + 10, -1), jnp.where(t >= 6, row + 4, -1)))

    load.wait()

    half = 4096

    def widen(i, _):
        span = pl.ds(pl.multiple_of(i * half, half), half)
        rows32[:, span] = slab[:, span].astype(F32)
        return 0

    lax.fori_loop(0, slab.shape[1] // half, widen, 0)
    first = 4 * lax.rem(h, 4)
    blocks = data.shape[1]
    for c in range(PART):
        data[c] = rows32[pl.ds(first + c, 1), :].reshape(blocks, BLK).astype(BF16)

    chunk = 128
    ones = jnp.ones((blocks, BLK), BF16)

    def local_sums(m, _):
        base = pl.multiple_of(m * chunk, chunk)
        at = lax.broadcasted_iota(jnp.int32, (chunk, blocks), 0) + base

        def spread(which):
            total = jnp.zeros((chunk, blocks), F32)
            for code in codes:
                total = total + jnp.where(at == code[which], code[0], 0.0)
            return total.astype(BF16)

        def dot(a, b):
            return jnp.dot(a, b, preferred_element_type=F32)

        main = spread(1)
        counts = dot(main, ones).reshape(chunk // ROWS, ROWS, BLK)
        r = lax.broadcasted_iota(jnp.int32, counts.shape, 1)
        lane = lax.broadcasted_iota(jnp.int32, counts.shape, 2)
        counts = jnp.sum(jnp.where(r == lane, counts, 0.0), axis=1, keepdims=True)
        counts = jnp.where(r == TILES, counts, 0.0).reshape(chunk, BLK)
        span = pl.ds(base, chunk)
        part[span, 0:BLK] = (dot(main, data[0]) + dot(spread(2), data[3])).astype(BF16)
        part[span, BLK:2 * BLK] = (dot(main, data[1]) + dot(spread(3), data[3])).astype(BF16)
        part[span, 2 * BLK:] = (dot(main, data[2]) + counts).astype(BF16)
        return 0

    lax.fori_loop(0, LON * ROWS // chunk, local_sums, 0)
    for copy in own:
        copy.wait()

    pl.semaphore_wait(barrier, len(peers))

    def remote(src, dst, ss, rs, peer):
        return pltpu.make_async_remote_copy(
            src_ref=src, dst_ref=dst, send_sem=ss, recv_sem=rs, device_id=peer, device_id_type=MESH
        )

    order = [1, 2, 3, 0]
    other = lax.rem(x + 1, NX)

    def piece(side, d):
        return pl.ds(pl.multiple_of((side * QA + lax.rem(q + d, QA)) * PIECE, PIECE), PIECE)

    x_copies = {}
    for d in order:
        x_copies[d] = remote(part.at[piece(other, d)], xin.at[d], xs.at[d], xr.at[d], x_peer)
        x_copies[d].start()
    a_copies = {}
    for d in order:
        x_copies[d].wait_recv()
        total = part[piece(x, d), :].astype(F32) + xin[d].astype(F32)
        mine[d] = total.astype(BF16)
        if d:
            a_copies[d] = remote(mine.at[d], ain.at[d], as_.at[d], ar.at[d], a_peer[d])
            a_copies[d].start()

    w_copies = []
    for d in range(1, NH):
        to = h_index[d]
        lane = pl.ds(pl.multiple_of(lax.rem(to, TILES) * BLK, BLK), BLK)
        w_copies.append((
            remote(latent.at[:, lane], lat_all.at[h], ls.at[d], lr.at[d], h_peer[d]),
            remote(we_all.at[h], we_all.at[h], es.at[d], er.at[d], h_peer[d]),
            remote(w_all.at[h], w_all.at[h], ws.at[d], wr.at[d], h_peer[d]),
        ))

        @pl.when(to < TILES)
        def _():
            for copy in w_copies[d - 1]:
                copy.start()

    for d in range(1, QA):
        a_copies[d].wait_recv()
    for k in range(KB):
        at = pl.ds(k * ROWS, ROWS)
        total = mine[0, at].astype(F32)
        for d in range(1, QA):
            total = total + ain[d, at].astype(F32)
        summed[at] = total.astype(BF16)
    b_copies = {}
    for d in (4, 3, 5, 2, 6, 1, 7):
        at = pl.ds(pl.multiple_of(lax.rem(g + d, KB) * ROWS, ROWS), ROWS)
        b_copies[d] = remote(summed.at[at], bin_.at[d], bs.at[d], br.at[d], b_peer[d])
        b_copies[d].start()

    @pl.when(h < TILES)
    def _():
        lane = pl.ds(pl.multiple_of(lax.rem(h, TILES) * BLK, BLK), BLK)
        copy = pltpu.make_async_copy(latent.at[:, lane], lat_all.at[h], load_sem)
        copy.start()
        copy.wait()
        for d in range(1, NH):
            for copy in w_copies[d - 1]:
                copy.wait_recv()

    total = summed[pl.ds(pl.multiple_of(g * ROWS, ROWS), ROWS)].astype(F32)
    for d in range(1, KB):
        b_copies[d].wait_recv()
        total = total + bin_[d].astype(F32)

    tiles_out[...] = jnp.zeros(tiles_out.shape, F32)
    for i in range(TILES):
        for c in range(3):
            tiles_out[i, c:c + 1] = total[i:i + 1, c * BLK:(c + 1) * BLK]
        r, c = (10 + i, 0) if i < 6 else (4 + i, 1)
        tiles_out[i, 3:4] = total[r:r + 1, c * BLK:(c + 1) * BLK]
        tiles_out[i, 4:5] = jnp.broadcast_to(total[10:11, 2 * BLK + i:2 * BLK + i + 1], (1, BLK))
    t_copies = []
    for d in range(1, NH):
        to = h_index[d]
        t_copies.append(remote(tiles_out.at[lax.rem(to, TILES)], tiles_in.at[h], ts.at[d], tr.at[d], h_peer[d]))

        @pl.when(to < TILES)
        def _():
            t_copies[d - 1].start()

    o_copies = []
    me_lane = pl.ds(pl.multiple_of(lax.rem(h, TILES) * BLK, BLK), BLK)
    for d in range(1, NH):
        to = h_index[d]
        src = out_all.at[pl.ds(pl.multiple_of(to * share, share), share)]
        o_copies.append(remote(src, out.at[:, me_lane], os_.at[d], or_.at[d], h_peer[d]))

    @pl.when(h < TILES)
    def _():
        tiles_in[h] = tiles_out[lax.rem(h, TILES)]
        for copy in t_copies:
            copy.wait_recv()
        sums = tiles_in[...]
        number = sums[0, 4:5]
        sums = sums[:, 0:PART].reshape(NH * PART, BLK)
        extra = jnp.where(lax.broadcasted_iota(jnp.int32, (BLK - NH * PART, BLK), 0) < 3, number, 0.0)
        sums = jnp.concatenate([sums, extra], axis=0)
        we = we_all[...].reshape(NH * share, BLK)
        smooth = jnp.zeros((NH * share, BLK), F32)
        for _ in range(3):
            piece16 = sums.astype(BF16)
            smooth = smooth + jnp.dot(we, piece16, preferred_element_type=F32)
            sums = sums - piece16.astype(F32)
        lat = lat_all[...].reshape(NH * share, BLK).astype(F32)
        mixed = (lat + scale * smooth).astype(BF16).astype(F32)
        mean_square = jnp.mean(mixed * mixed, axis=0, keepdims=True)
        normed = (mixed * lax.rsqrt(mean_square + 1e-05) * gain_t[...]).astype(BF16)
        wide = w_gate.shape[1]
        gate = jnp.dot(w_all[:, 0].reshape(NH * share, wide), normed, preferred_element_type=F32)
        up = jnp.dot(w_all[:, 1].reshape(NH * share, wide), normed, preferred_element_type=F32)
        hidden = (gate / (1.0 + jnp.exp(-gate)) * up).astype(BF16)
        down = w_all[:, 2].reshape(NH * share, wide)
        value = lax.dot_general(down, hidden, (((0,), (0,)), ((), ())), preferred_element_type=F32)
        out_all[...] = (lat + value).astype(BF16)
        for copy in o_copies:
            copy.start()
        out[:, me_lane] = out_all[pl.ds(pl.multiple_of(h * share, share), share)]

    for d in range(1, NH):
        source = lax.rem(h + NH - d, NH)

        @pl.when(source < TILES)
        def _():
            o_copies[d - 1].wait_recv()

    for d in range(QA):
        x_copies[d].wait_send()
    for d in range(1, QA):
        a_copies[d].wait_send()
    for d in range(1, KB):
        b_copies[d].wait_send()
    for d in range(1, NH):

        @pl.when(h_index[d] < TILES)
        def _():
            for copy in w_copies[d - 1]:
                copy.wait_send()
            t_copies[d - 1].wait_send()

    @pl.when(h < TILES)
    def _():
        for copy in o_copies:
            copy.wait_send()


def local(observations, block_owner, block_tile, embed_weight, embed_bias, mesh_latent, norm_gain, w_gate, w_up, w_down):
    blocks = block_tile.shape[0]
    rows = observations.shape[0]
    share = embed_weight.shape[1]
    nodes = mesh_latent.shape[0]
    lat = norm_gain.shape[0]
    pieces, rest = [], embed_bias
    for _ in range(3):
        pieces.append(rest.astype(BF16))
        rest = rest - pieces[-1].astype(F32)
    spare = jnp.zeros((share, BLK - embed_weight.shape[0] - 3), BF16)
    weight = jnp.concatenate([embed_weight.T] + [p[:, None] for p in pieces] + [spare], axis=1)
    vmem = pl.BlockSpec(memory_space=pltpu.VMEM)
    anywhere = pl.BlockSpec(memory_space=pl.ANY)
    dma = pltpu.SemaphoreType.DMA
    out = pl.pallas_call(
        functools.partial(kernel, math.sqrt(TILES / blocks)),
        out_shape=jax.ShapeDtypeStruct((share, nodes), BF16),
        in_specs=[anywhere, vmem, vmem, vmem, vmem, vmem, anywhere, anywhere, anywhere],
        out_specs=vmem,
        scratch_shapes=[
            pltpu.VMEM((16, rows), BF16),
            pltpu.VMEM((16, rows), F32),
            pltpu.VMEM((PART, blocks, BLK), BF16),
            pltpu.VMEM((LON * ROWS, WIDE), BF16),
            pltpu.VMEM((QA, PIECE, WIDE), BF16),
            pltpu.VMEM((QA, PIECE, WIDE), BF16),
            pltpu.VMEM((QA, PIECE, WIDE), BF16),
            pltpu.VMEM((PIECE, WIDE), BF16),
            pltpu.VMEM((KB, ROWS, WIDE), BF16),
            pltpu.VMEM((TILES, 8, BLK), F32),
            pltpu.VMEM((NH, 8, BLK), F32),
            pltpu.VMEM((NH, 3, share, lat), BF16),
            pltpu.VMEM((NH, share, BLK), BF16),
            pltpu.VMEM((NH, share, BLK), BF16),
            pltpu.VMEM((lat, BLK), F32),
            pltpu.VMEM((lat, BLK), BF16),
            dma, dma((4,)),
            dma((QA,)), dma((QA,)), dma((QA,)), dma((QA,)), dma((KB,)), dma((KB,)),
            dma((NH,)), dma((NH,)), dma((NH,)), dma((NH,)), dma((NH,)), dma((NH,)),
            dma((NH,)), dma((NH,)), dma((NH,)), dma((NH,)),
        ],
        compiler_params=pltpu.CompilerParams(collective_id=0, has_side_effects=True, vmem_limit_bytes=40 * 2**20),
    )(
        observations.T, block_owner.T, block_tile[None, :], weight, mesh_latent.T, norm_gain[None, :],
        w_gate.T, w_up.T, w_down,
    )
    return out.T


def solution(mesh):
    return jax.shard_map(
        local,
        mesh=mesh,
        in_specs=(
            P("lon", None),
            P("lon", None),
            P("lon"),
            P(None, "hid"),
            P("hid"),
            P("lon", "hid"),
            P(),
            P(None, "hid"),
            P(None, "hid"),
            P("hid", None),
        ),
        out_specs=P("lon", "hid"),
        check_vma=False,
    )
```

time: 325 us -> 87.5 us (0.27)
  blocking collectives: 132 us -> 0 us
  waiting for transfers between devices: 90.8 us -> 0 us
  Pallas kernels: 0 us -> 77.1 us
  starting transfers between devices: 73.1 us -> 0 us
  between operations: 14.2 us -> 0.03 us
    all_gather x4 -> x0, blocking collectives: 89 us -> none  [the longest x1 25.9 us: local(): wg = lax.all_gather(w_gate, 'hid', axis=1, tiled=True)]
    reduce_scatter x1 -> x0, waiting for transfers between devices: 84.3 us -> none  [local(): lax.psum_scatter(sums.reshape(lon * PAD, part * BLK), 'lon', scatter_dime...]
    pallas_call x0 -> x1, Pallas kernels: none -> 77.1 us  [local(): pl.pallas_call(functools.partial(kernel, math.sqrt(TILES / blocks)), out_...]
    all_to_all x2 -> x0, starting transfers between devices: 73.1 us -> none  [the longest x1 55.6 us: local(): lax.all_to_all(nodes, 'hid', split_axis=1, concat_axis=0, tiled=True)]
    unnamed x1 -> x0, blocking collectives: 32.7 us -> none
    all_to_all x1 -> x0, blocking collectives: 10.5 us -> none  [local(): return lax.all_to_all(out, 'hid', split_axis=1, concat_axis=0, tiled=True)]
    all_to_all x2 -> x0, waiting for transfers between devices: 6.48 us -> none  [the longest x1 6.48 us: local(): lax.all_to_all(nodes, 'hid', split_axis=1, concat_axis=0, tiled=True)]
    unnamed x17, local copies, waits for them, and re-layouts: 2.37 us -> 8.02 us
  transfers between devices with their start and end apart: 3 -> 0, of which waited for: 2 -> 0; matrix products, arithmetic and copies ran while one was open for 1% -> 0% of each run, Pallas kernels for 0% -> 0%
where the time goes in v2:
time: 87.5 us; the launch traced here: 86.9 us
  Pallas kernels  77.1 us (88%)
  local copies, waits for them, and re-layouts  9.12 us (10%)
    pallas_call x1, Pallas kernels, local(): pl.pallas_call(functools.partial(kernel, math.sqrt(TILES / blocks)), out_...  77.1 us
    unnamed x17, local copies, waits for them, and re-layouts  8.02 us

profile of v2, /device:TPU:1, one launch (start us, length us, event | category | flops | bytes accessed | tf_op | source)
XLA Modules:
  0.0 86.9 jit_solution(3505133794239847630)
XLA Ops:
  0.0 0.7 convert_bitcast_fusion
  0.7 0.1 copy.13
  0.8 0.1 copy.12
  0.9 0.1 copy.11
  1.0 0.8 concatenate.3.weight
  1.8 0.0 copy-start
  1.8 2.2 %copy-done = bf16[32768,64]{0,1:T(8,128)(2,1)S(1)} copy-done((bf16[32768,64]{0,1:T(8,128)(2,1)S(1)}, bf16[32768,64]{0,1:T(8,128)(2,1)}, u32[]{:S(2)}) %copy-start) | copy-done | bytes 4194328
  4.0 0.0 copy-start.1
  4.0 0.9 %copy-done.1 = bf16[1280,32]{0,1:T(8,128)(2,1)S(1)} copy-done((bf16[1280,32]{0,1:T(8,128)(2,1)S(1)}, bf16[1280,32]{0,1:T(8,128)(2,1)}, u32[]{:S(2)}) %copy-start.1) | copy-done | bytes 81944
  4.9 0.0 copy-start.2
  4.9 0.8 copy-done.2
  5.7 0.0 copy-start.3
  5.7 0.8 copy-done.3
  6.4 0.0 copy-start.4
  6.4 0.8 copy-done.4
  7.2 0.0 copy-start.5
  7.2 0.7 copy-done.5
  7.9 0.0 copy-start.6
  7.9 0.7 copy-done.6
  8.6 0.0 copy-start.7
  8.6 0.7 copy-done.7
  9.2 77.1 %shard_map.100 = bf16[32,1280]{1,0:T(8,128)(2,1)S(1)} custom-call(bf16[64,32768]{1,0:T(8,128)(2,1)S(1)} %bitcast.15, s32[1,256]{1,0:T(1,128)S(1)} %bitcast.21, s32[1,256]{1,0:T(1,128)S(1)} %bitcast.22, bf16[32,128]{1,0:T(8,128)(2,1)S(1)} %concatenate.3.weight, bf16[32,1280]{1,0:T(8,128)(2,1)S(1)} %bitcast.17, f32[1,512]{1,0:T(1,128)S(1)} %bitcast.20, ...), custom_call_target="tpu_custom_call" | custom-call | tf_op jit(solution)/shard_map/pallas_call | solution.py:294
  86.3 0.6 copy.15
  (1 shorter events, 0.0 us)
Async XLA Ops:
  1.8 2.2 %copy-start = (bf16[32768,64]{0,1:T(8,128)(2,1)S(1)}, bf16[32768,64]{0,1:T(8,128)(2,1)}, u32[]{:S(2)}) copy-start(bf16[32768,64]{0,1:T(8,128)(2,1)} %param.10) | copy-start | bytes 12582916
  4.0 0.9 %copy-start.1 = (bf16[1280,32]{0,1:T(8,128)(2,1)S(1)}, bf16[1280,32]{0,1:T(8,128)(2,1)}, u32[]{:S(2)}) copy-start(bf16[1280,32]{0,1:T(8,128)(2,1)} %param.15) | copy-start | bytes 245764
  4.9 0.8 copy-start.2
  5.7 0.8 copy-start.3
  6.4 0.8 copy-start.4
  7.2 0.7 copy-start.5
  7.9 0.7 copy-start.6
  8.6 0.7 copy-start.7

commit v3 on v2

v3 whole, which is shorter than its diff:
```python
import functools
import math

import jax
import jax.numpy as jnp
from jax import lax
from jax.experimental import pallas as pl
from jax.experimental.pallas import tpu as pltpu
from jax.sharding import PartitionSpec as P

MESH = pl.DeviceIdType.MESH
BLK = 128
NX = 2
NZ = 32
NH = 16
NY = 4
LON = NX * NZ
QA = 4
KB = NZ // QA
TILES = 10
ROWS = 16
PART = 4
WIDE = 3 * BLK
PIECE = KB * ROWS
SPOTS = (4, 3, 5, 2, 6, 1, 7, 0)
F32 = jnp.float32
BF16 = jnp.bfloat16


def kernel(
    scale,
    obs, owner_in, tile_in, weight, bias_in, latent, gain_in, w_gate, w_up, w_down,
    out,
    owner, tile, bias, gain, we_own, slab, rows32, data, part, xin, mine, ain, summed, bin_,
    tiles_out, tiles_in, w_all, down_t, we_all, lat_all, gain_t, out_all,
    load_sem, own_sem, xs, xr, as_, ar, bs, br, wys, wyr, wxs, wxr, es, er, ls, lr, ts, tr, os_, or_,
):
    lon = lax.axis_index("lon")
    h = lax.axis_index("hid")
    x = lon // NZ
    z = lax.rem(lon, NZ)
    core = lax.rem(h, 2)
    y = lax.rem(h // 2, NY)
    xh = h // (2 * NY)
    off = 2 * core
    v = lax.rem(z + off, NZ)
    g = v // QA
    q = lax.rem(v, QA)

    def at_v(value):
        return (x * NZ + lax.rem(value - off + NZ, NZ), h)

    def at_hid(xh, y, core):
        return (lon, (xh * NY + y) * 2 + core)

    def active(to):
        return (lax.rem(to, 2) == 0) | (lax.rem(to // 2, NY) == 0)

    def tile_of(to):
        return (to // (2 * NY)) * (NY + 1) + jnp.where(lax.rem(to, 2) == 0, lax.rem(to // 2, NY), NY)

    x_peer = (lax.rem(x + 1, NX) * NZ + z, h)
    a_peer = [at_v(g * QA + lax.rem(q + d, QA)) for d in range(QA)]
    b_peer = [at_v(lax.rem(g + d, KB) * QA + q) for d in range(KB)]
    h_index = [lax.rem(h + d, NH) for d in range(NH)]
    h_peer = [(lon, i) for i in h_index]

    barrier = pltpu.get_barrier_semaphore()
    peers = [x_peer] + a_peer[1:] + b_peer[1:] + h_peer[1:]
    for peer in peers:
        pl.semaphore_signal(barrier, inc=1, device_id=peer, device_id_type=MESH)

    load = pltpu.make_async_copy(obs.at[pl.ds(pl.multiple_of((h // 4) * 16, 16), 16)], slab, load_sem)
    load.start()
    share = w_down.shape[0]
    place = core * (2 * NY) + xh * NY + y
    own = [
        pltpu.make_async_copy(owner_in, owner, own_sem.at[0]),
        pltpu.make_async_copy(tile_in, tile, own_sem.at[1]),
        pltpu.make_async_copy(w_gate, w_all.at[place, 0], own_sem.at[2]),
        pltpu.make_async_copy(w_up, w_all.at[place, 1], own_sem.at[3]),
        pltpu.make_async_copy(w_down, w_all.at[place, 2], own_sem.at[4]),
        pltpu.make_async_copy(bias_in, bias, own_sem.at[5]),
        pltpu.make_async_copy(gain_in, gain, own_sem.at[6]),
        pltpu.make_async_copy(weight, we_own, own_sem.at[7]),
    ]
    for copy in own:
        copy.start()
    own[0].wait()
    own[1].wait()

    codes = []
    for step, weigh in ((0, 1.0), (-1, 0.5), (1, 0.5)):
        t = tile[...] + step
        o = owner[...]
        o = jnp.where(t < 0, (o + LON - 1) & (LON - 1), jnp.where(t >= TILES, (o + 1) & (LON - 1), o))
        t = jnp.where(t < 0, TILES - 1, jnp.where(t >= TILES, 0, t))
        u = ((o & (NZ - 1)) + off) & (NZ - 1)
        side = (o >> 5) ^ x
        dq = ((u & (QA - 1)) - q) & (QA - 1)
        m = (((u >> 2) - g) & (KB - 1)) - KB // 2
        spot = jnp.where(m < 0, -2 * m - 1, 2 * m)
        codes.append((weigh, ((side * QA + dq) * KB + spot) * ROWS + t))

    blocks = data.shape[0]
    load.wait()

    def widen(b, _):
        rows = pl.ds(pl.multiple_of(b * 16, 16), 16)
        rows32[rows] = slab[:, pl.ds(pl.multiple_of(b * BLK, BLK), BLK)].astype(F32)
        return 0

    lax.fori_loop(0, blocks, widen, 0, unroll=16)
    first = PART * lax.rem(h, 4)
    for c in range(PART):
        data[:, c * BLK:(c + 1) * BLK] = rows32[pl.ds(first + c, blocks, stride=16), :].astype(BF16)
    data[:, PART * BLK:] = jnp.ones((blocks, BLK), BF16)

    def sums_of(side, d):
        at = lax.broadcasted_iota(jnp.int32, (PIECE, blocks), 0) + (side * QA + d) * PIECE
        spread = jnp.zeros((PIECE, blocks), F32)
        for weigh, code in codes:
            spread = jnp.where(at == code, weigh, spread)
        full = jnp.dot(spread.astype(BF16), data[...], preferred_element_type=F32)
        fourth = full[:, 3 * BLK:4 * BLK]
        r = lax.rem(lax.broadcasted_iota(jnp.int32, (PIECE, BLK), 0), ROWS)
        lane = lax.broadcasted_iota(jnp.int32, (PIECE, BLK), 1)
        counts = jnp.where(r == lane, full[:, 4 * BLK:], 0.0).reshape(KB, ROWS, BLK)
        counts = jnp.broadcast_to(jnp.sum(counts, axis=1, keepdims=True), (KB, ROWS, BLK)).reshape(PIECE, BLK)
        return [
            jnp.where(r < TILES, full[:, 0:BLK], pltpu.roll(fourth, 10, 0)),
            jnp.where(r < TILES, full[:, BLK:2 * BLK], pltpu.roll(fourth, 4, 0)),
            jnp.where(r < TILES, full[:, 2 * BLK:3 * BLK], counts),
        ]

    order = [1, 2, 3, 0]
    for d in order:
        for c, value in enumerate(sums_of(1, d)):
            part[d, :, c * BLK:(c + 1) * BLK] = value.astype(BF16)

    def remote(src, dst, ss, rs, peer):
        return pltpu.make_async_remote_copy(
            src_ref=src, dst_ref=dst, send_sem=ss, recv_sem=rs, device_id=peer, device_id_type=MESH
        )

    pl.semaphore_wait(barrier, len(peers))
    x_copies = {}
    for d in order:
        x_copies[d] = remote(part.at[d], xin.at[d], xs.at[d], xr.at[d], x_peer)
        x_copies[d].start()
    for copy in own[2:]:
        copy.wait()
    wy_copies = []
    for d in range(1, NY):
        ref = w_all.at[place]
        wy_copies.append(remote(ref, ref, wys.at[d], wyr.at[d], at_hid(xh, lax.rem(y + d, NY), core)))
        wy_copies[-1].start()

    half = PIECE // 2
    a_copies = {}
    for d in order:
        values = sums_of(0, d)
        x_copies[d].wait_recv()
        for c, value in enumerate(values):
            lanes = slice(c * BLK, (c + 1) * BLK)
            mine[d, :, lanes] = (value + xin[d, :, lanes].astype(F32)).astype(BF16)
        if d:
            for i in range(2):
                at = pl.ds(i * half, half)
                a_copies[d, i] = remote(mine.at[d, at], ain.at[d, at], as_.at[d, i], ar.at[d, i], a_peer[d])
            a_copies[d, 0].start()
    for d in range(1, QA):
        a_copies[d, 1].start()

    r = lax.broadcasted_iota(jnp.int32, (share, BLK), 0)
    lane = lax.broadcasted_iota(jnp.int32, (share, BLK), 1)
    spare = jnp.zeros((share, BLK - share), F32)
    row = jnp.concatenate([jnp.broadcast_to(bias[...], (share, share)), spare], axis=1)
    rest = jnp.sum(jnp.where(r == lane, row, 0.0), axis=1, keepdims=True)
    channels = NH * PART
    we_wide = jnp.concatenate([we_own[...].astype(F32), jnp.zeros((share, BLK - channels), F32)], axis=1)
    for i in range(3):
        digit = rest.astype(BF16).astype(F32)
        we_wide = jnp.where(lane == channels + i, digit, we_wide)
        rest = rest - digit
    we_all[h] = we_wide.astype(BF16)

    for copy in wy_copies:
        copy.wait_recv()
    ref = w_all.at[pl.ds(core * (2 * NY) + xh * NY, NY)]
    wx_copy = remote(ref, ref, wxs.at[0], wxr.at[0], at_hid(1 - xh, y, core))
    wx_copy.start()

    small = []
    for d in range(1, NH):
        to = h_index[d]
        lanes = pl.ds(pl.multiple_of(tile_of(to) * BLK, BLK), BLK)
        small.append((
            remote(latent.at[:, lanes], lat_all.at[h], ls.at[d], lr.at[d], h_peer[d]),
            remote(we_all.at[h], we_all.at[h], es.at[d], er.at[d], h_peer[d]),
        ))

        @pl.when(active(to))
        def _():
            for copy in small[d - 1]:
                copy.start()

    b_copies = {}
    for i in range(2):
        for d in range(1, QA):
            a_copies[d, i].wait_recv()
        at = pl.ds(i * half, half)
        total = mine[0, at].astype(F32)
        for d in range(1, QA):
            total = total + ain[d, at].astype(F32)
        summed[at] = total.astype(BF16)
        for spot in range(i * KB // 2, (i + 1) * KB // 2):
            d = SPOTS[spot]
            if d:
                rows = pl.ds(spot * ROWS, ROWS)
                b_copies[d] = remote(summed.at[rows], bin_.at[d], bs.at[d], br.at[d], b_peer[d])
                b_copies[d].start()
    my_lanes = pl.ds(pl.multiple_of(tile_of(h) * BLK, BLK), BLK)
    wx_copy.wait_recv()
    ref = w_all.at[pl.ds(core * (2 * NY), 2 * NY)]
    wc_copy = remote(ref, ref, wxs.at[1], wxr.at[1], at_hid(xh, y, 1 - core))
    wc_copy.start()
    gain_t[...] = jnp.broadcast_to(gain[...], (BLK, gain.shape[1])).T

    @pl.when(active(h))
    def _():
        copy = pltpu.make_async_copy(latent.at[:, my_lanes], lat_all.at[h], load_sem)
        copy.start()
        copy.wait()
        for copies in small:
            for copy in copies:
                copy.wait_recv()

    wide = w_gate.shape[1]
    wc_copy.wait_recv()
    down_t[...] = w_all[:, 2].reshape(NH * share, wide).T
    total = summed[pl.ds((KB - 1) * ROWS, ROWS)].astype(F32)
    for d in (1, 7, 2, 6, 3, 5, 4):
        b_copies[d].wait_recv()
        total = total + bin_[d].astype(F32)
    for i in range(TILES):
        for c in range(3):
            tiles_out[i, c:c + 1] = total[i:i + 1, c * BLK:(c + 1) * BLK]
        r, c = (10 + i, 0) if i < 6 else (4 + i, 1)
        tiles_out[i, 3:4] = total[r:r + 1, c * BLK:(c + 1) * BLK]
        tiles_out[i, 4:8] = jnp.broadcast_to(total[10:11, 2 * BLK + i:2 * BLK + i + 1], (4, BLK))
    t_copies = []
    for d in range(1, NH):
        to = h_index[d]
        t_copies.append(remote(tiles_out.at[tile_of(to)], tiles_in.at[h], ts.at[d], tr.at[d], h_peer[d]))

        @pl.when(active(to))
        def _():
            t_copies[d - 1].start()

    o_copies = []
    for d in range(1, NH):
        to = h_index[d]
        src = out_all.at[pl.ds(pl.multiple_of(to * share, share), share)]
        o_copies.append(remote(src, out.at[:, my_lanes], os_.at[d], or_.at[d], h_peer[d]))

    @pl.when(active(h))
    def _():
        tiles_in[h] = tiles_out[tile_of(h)]
        for copy in t_copies:
            copy.wait_recv()
        sums = tiles_in[...]
        number = sums[0, 4:5]
        sums = sums[:, 0:PART].reshape(channels, BLK)
        extra = jnp.where(lax.broadcasted_iota(jnp.int32, (BLK - channels, BLK), 0) < 3, number, 0.0)
        sums = jnp.concatenate([sums, extra], axis=0)
        we = we_all[...].reshape(NH * share, BLK)
        smooth = jnp.zeros((NH * share, BLK), F32)
        for _ in range(3):
            digit = sums.astype(BF16)
            smooth = smooth + jnp.dot(we, digit, preferred_element_type=F32)
            sums = sums - digit.astype(F32)
        lat = lat_all[...].reshape(NH * share, BLK).astype(F32)
        mixed = (lat + scale * smooth).astype(BF16).astype(F32)
        mean_square = jnp.mean(mixed * mixed, axis=0, keepdims=True)
        normed = (mixed * lax.rsqrt(mean_square + 1e-05) * gain_t[...]).astype(BF16)
        gate = jnp.dot(w_all[:, 0].reshape(NH * share, wide), normed, preferred_element_type=F32)
        up = jnp.dot(w_all[:, 1].reshape(NH * share, wide), normed, preferred_element_type=F32)
        hidden = (gate / (1.0 + jnp.exp(-gate)) * up).astype(BF16)
        value = jnp.dot(down_t[...], hidden, preferred_element_type=F32)
        out_all[...] = (lat + value).astype(BF16)
        for copy in o_copies:
            copy.start()
        copy = pltpu.make_async_copy(
            out_all.at[pl.ds(pl.multiple_of(h * share, share), share)], out.at[:, my_lanes], load_sem
        )
        copy.start()
        copy.wait()

    for d in range(1, NH):

        @pl.when(active(lax.rem(h + NH - d, NH)))
        def _():
            o_copies[d - 1].wait_recv()

    sent = list(x_copies.values()) + list(a_copies.values()) + list(b_copies.values())
    for copy in sent + wy_copies + [wx_copy, wc_copy]:
        copy.wait_send()
    for d in range(1, NH):

        @pl.when(active(h_index[d]))
        def _():
            for copy in small[d - 1]:
                copy.wait_send()
            t_copies[d - 1].wait_send()

    @pl.when(active(h))
    def _():
        for copy in o_copies:
            copy.wait_send()


def local(observations, block_owner, block_tile, embed_weight, embed_bias, mesh_latent, norm_gain, w_gate, w_up, w_down):
    blocks = block_tile.shape[0]
    rows = observations.shape[0]
    share = embed_weight.shape[1]
    nodes = mesh_latent.shape[0]
    lat = norm_gain.shape[0]
    hbm = pl.BlockSpec(memory_space=pltpu.HBM)
    dma = pltpu.SemaphoreType.DMA
    out = pl.pallas_call(
        functools.partial(kernel, math.sqrt(TILES / blocks)),
        out_shape=jax.ShapeDtypeStruct((share, nodes), BF16),
        in_specs=[hbm] * 10,
        out_specs=hbm,
        scratch_shapes=[
            pltpu.VMEM((1, blocks), jnp.int32),
            pltpu.VMEM((1, blocks), jnp.int32),
            pltpu.VMEM((1, share), F32),
            pltpu.VMEM((1, lat), F32),
            pltpu.VMEM((share, NH * PART), BF16),
            pltpu.VMEM((16, rows), BF16),
            pltpu.VMEM((blocks * 16, BLK), F32),
            pltpu.VMEM((blocks, (PART + 1) * BLK), BF16),
            pltpu.VMEM((QA, PIECE, WIDE), BF16),
            pltpu.VMEM((QA, PIECE, WIDE), BF16),
            pltpu.VMEM((QA, PIECE, WIDE), BF16),
            pltpu.VMEM((QA, PIECE, WIDE), BF16),
            pltpu.VMEM((PIECE, WIDE), BF16),
            pltpu.VMEM((KB, ROWS, WIDE), BF16),
            pltpu.VMEM((TILES, 8, BLK), F32),
            pltpu.VMEM((NH, 8, BLK), F32),
            pltpu.VMEM((NH, 3, share, lat), BF16),
            pltpu.VMEM((lat, NH * share), BF16),
            pltpu.VMEM((NH, share, BLK), BF16),
            pltpu.VMEM((NH, share, BLK), BF16),
            pltpu.VMEM((lat, BLK), F32),
            pltpu.VMEM((lat, BLK), BF16),
            dma, dma((8,)),
            dma((QA,)), dma((QA,)), dma((QA, 2)), dma((QA, 2)), dma((KB,)), dma((KB,)),
            dma((NY,)), dma((NY,)), dma((2,)), dma((2,)),
            dma((NH,)), dma((NH,)), dma((NH,)), dma((NH,)), dma((NH,)), dma((NH,)), dma((NH,)), dma((NH,)),
        ],
        compiler_params=pltpu.CompilerParams(collective_id=0, has_side_effects=True, vmem_limit_bytes=64 * 2**20),
    )(
        observations.T, block_owner.T, block_tile[None, :], embed_weight.T, embed_bias[None, :], mesh_latent.T, norm_gain[None, :],
        w_gate.T, w_up.T, w_down,
    )
    return out.T


def solution(mesh):
    return jax.shard_map(
        local,
        mesh=mesh,
        in_specs=(
            P("lon", None),
            P("lon", None),
            P("lon"),
            P(None, "hid"),
            P("hid"),
            P("lon", "hid"),
            P(),
            P(None, "hid"),
            P(None, "hid"),
            P("hid", None),
        ),
        out_specs=P("lon", "hid"),
        check_vma=False,
    )
```

time: 87.5 us -> 68.9 us (0.79)
  Pallas kernels: 77.1 us -> 67.2 us
  local copies, waits for them, and re-layouts: 9.12 us -> 1.53 us
    pallas_call x1, Pallas kernels: 77.1 us -> 67.2 us  [local(): pl.pallas_call(functools.partial(kernel, math.sqrt(TILES / blocks)), out_...]
    unnamed x17 -> x1, local copies, waits for them, and re-layouts: 8.02 us -> 1.53 us
where the time goes in v3:
time: 68.9 us; the launch traced here: 68.7 us
  Pallas kernels  67.2 us (98%)
  local copies, waits for them, and re-layouts  1.53 us (2%)
    pallas_call x1, Pallas kernels, local(): pl.pallas_call(functools.partial(kernel, math.sqrt(TILES / blocks)), out_...  67.2 us
    unnamed x1, local copies, waits for them, and re-layouts  1.53 us

profile of v3, /device:TPU:1, one launch (start us, length us, event | category | flops | bytes accessed | tf_op | source)
XLA Modules:
  0.0 68.7 jit_solution(3681190971241223305)
XLA Ops:
  0.0 67.2 %shard_map.100 = bf16[32,1280]{1,0:T(8,128)(2,1)} custom-call(bf16[64,32768]{1,0:T(8,128)(2,1)} %bitcast.10, s32[1,256]{1,0:T(1,128)} %bitcast.17, s32[1,256]{1,0:T(1,128)} %bitcast.18, bf16[32,64]{1,0:T(8,128)(2,1)} %bitcast.15, f32[1,32]{1,0:T(1,128)} %bitcast.19, bf16[32,1280]{1,0:T(8,128)(2,1)} %bitcast.12, f32[1,512]{1,0:T(1,128)} %bitcast.16, ...), custom_call_target="tpu_custom_call" | custom-call | tf_op jit(solution)/shard_map/pallas_call | solution.py:331
  67.2 1.5 %copy.12 = bf16[1280,32]{0,1:T(8,128)(2,1)} copy(bf16[1280,32]{0,1:T(8,128)(2,1)} %bitcast.11) | data formatting | bytes 163840

commit v4 on v3

--- a/solution.py
+++ b/solution.py
@@ -19,10 +19,14 @@
 KB = NZ // QA
 TILES = 10
 ROWS = 16
-PART = 4
+PART = 8
+NG = NH // 2
+HALF = TILES // 2
 WIDE = 3 * BLK
 PIECE = KB * ROWS
-SPOTS = (4, 3, 5, 2, 6, 1, 7, 0)
+PHASES = KB // 2
+SPOTS = (2, 6, 1, 7, 3, 5, 4, 0)
+NEAR = (1, 7, 2, 6)
 F32 = jnp.float32
 BF16 = jnp.bfloat16
 
@@ -33,10 +37,11 @@
     out,
     owner, tile, bias, gain, we_own, slab, rows32, data, part, xin, mine, ain, summed, bin_,
     tiles_out, tiles_in, w_all, down_t, we_all, lat_all, gain_t, out_all,
-    load_sem, own_sem, xs, xr, as_, ar, bs, br, wys, wyr, wxs, wxr, es, er, ls, lr, ts, tr, os_, or_,
+    relay, load_sem, own_sem, xs, xr, as_, ar, bs, br, wys, wyr, wxs, wxr, es, er, ls, lr, ts, tr, os_, or_,
 ):
     lon = lax.axis_index("lon")
     h = lax.axis_index("hid")
+    group = lax.rem(h, NG)
     x = lon // NZ
     z = lax.rem(lon, NZ)
     core = lax.rem(h, 2)
@@ -66,11 +71,11 @@
     h_peer = [(lon, i) for i in h_index]
 
     barrier = pltpu.get_barrier_semaphore()
-    peers = [x_peer] + a_peer[1:] + b_peer[1:] + h_peer[1:]
+    peers = [x_peer] + a_peer[1:] + [b_peer[d] for d in NEAR] + h_peer[1:]
     for peer in peers:
         pl.semaphore_signal(barrier, inc=1, device_id=peer, device_id_type=MESH)
 
-    load = pltpu.make_async_copy(obs.at[pl.ds(pl.multiple_of((h // 4) * 16, 16), 16)], slab, load_sem)
+    load = pltpu.make_async_copy(obs.at[pl.ds(pl.multiple_of((group // 2) * 16, 16), 16)], slab, load_sem)
     load.start()
     share = w_down.shape[0]
     place = core * (2 * NY) + xh * NY + y
@@ -98,9 +103,13 @@
         u = ((o & (NZ - 1)) + off) & (NZ - 1)
         side = (o >> 5) ^ x
         dq = ((u & (QA - 1)) - q) & (QA - 1)
-        m = (((u >> 2) - g) & (KB - 1)) - KB // 2
-        spot = jnp.where(m < 0, -2 * m - 1, 2 * m)
-        codes.append((weigh, ((side * QA + dq) * KB + spot) * ROWS + t))
+        dk = ((u >> 2) - g) & (KB - 1)
+        spot = jnp.full(dk.shape, KB - 1, jnp.int32)
+        for place_of, d in enumerate(SPOTS[:-1]):
+            spot = jnp.where(dk == d, place_of, spot)
+        t = t - xh * HALF
+        row = (((side * PHASES + (spot >> 1)) * QA + dq) * 2 + (spot & 1)) * ROWS + t
+        codes.append((weigh, jnp.where((t >= 0) & (t < HALF), row, -1)))
 
     blocks = data.shape[0]
     load.wait()
@@ -111,32 +120,26 @@
         return 0
 
     lax.fori_loop(0, blocks, widen, 0, unroll=16)
-    first = PART * lax.rem(h, 4)
+    first = PART * lax.rem(group, 2)
     for c in range(PART):
         data[:, c * BLK:(c + 1) * BLK] = rows32[pl.ds(first + c, blocks, stride=16), :].astype(BF16)
     data[:, PART * BLK:] = jnp.ones((blocks, BLK), BF16)
 
-    def sums_of(side, d):
-        at = lax.broadcasted_iota(jnp.int32, (PIECE, blocks), 0) + (side * QA + d) * PIECE
+    def sums_of(side, p):
+        at = lax.broadcasted_iota(jnp.int32, (PIECE, blocks), 0) + (side * PHASES + p) * PIECE
         spread = jnp.zeros((PIECE, blocks), F32)
         for weigh, code in codes:
             spread = jnp.where(at == code, weigh, spread)
         full = jnp.dot(spread.astype(BF16), data[...], preferred_element_type=F32)
-        fourth = full[:, 3 * BLK:4 * BLK]
-        r = lax.rem(lax.broadcasted_iota(jnp.int32, (PIECE, BLK), 0), ROWS)
-        lane = lax.broadcasted_iota(jnp.int32, (PIECE, BLK), 1)
-        counts = jnp.where(r == lane, full[:, 4 * BLK:], 0.0).reshape(KB, ROWS, BLK)
-        counts = jnp.broadcast_to(jnp.sum(counts, axis=1, keepdims=True), (KB, ROWS, BLK)).reshape(PIECE, BLK)
+        cut = [full[:, i * BLK:(i + 1) * BLK] for i in range(PART + 1)]
         return [
-            jnp.where(r < TILES, full[:, 0:BLK], pltpu.roll(fourth, 10, 0)),
-            jnp.where(r < TILES, full[:, BLK:2 * BLK], pltpu.roll(fourth, 4, 0)),
-            jnp.where(r < TILES, full[:, 2 * BLK:3 * BLK], counts),
+            cut[i] + pltpu.roll(cut[i + 1], HALF, 0) + pltpu.roll(cut[i + 2], 2 * HALF, 0)
+            for i in range(0, PART + 1, 3)
         ]
 
-    order = [1, 2, 3, 0]
-    for d in order:
-        for c, value in enumerate(sums_of(1, d)):
-            part[d, :, c * BLK:(c + 1) * BLK] = value.astype(BF16)
+    for p in range(PHASES):
+        for c, value in enumerate(sums_of(1, p)):
+            part[p, :, c * BLK:(c + 1) * BLK] = value.astype(BF16)
 
     def remote(src, dst, ss, rs, peer):
         return pltpu.make_async_remote_copy(
@@ -145,9 +148,11 @@
 
     pl.semaphore_wait(barrier, len(peers))
     x_copies = {}
-    for d in order:
-        x_copies[d] = remote(part.at[d], xin.at[d], xs.at[d], xr.at[d], x_peer)
-        x_copies[d].start()
+    for p in range(PHASES):
+        x_copies[p] = remote(part.at[p], xin.at[p], xs.at[p], xr.at[p], x_peer)
+        x_copies[p].start()
+    for i, d in ((0, 7), (1, 1), (2, 6)):
+        pl.semaphore_signal(relay.at[i], inc=1, device_id=b_peer[d], device_id_type=MESH)
     for copy in own[2:]:
         copy.wait()
     wy_copies = []
@@ -156,40 +161,58 @@
         wy_copies.append(remote(ref, ref, wys.at[d], wyr.at[d], at_hid(xh, lax.rem(y + d, NY), core)))
         wy_copies[-1].start()
 
-    half = PIECE // 2
+    quarter = PIECE // QA
     a_copies = {}
-    for d in order:
-        values = sums_of(0, d)
-        x_copies[d].wait_recv()
+    for p in range(PHASES):
+        values = sums_of(0, p)
+        x_copies[p].wait_recv()
         for c, value in enumerate(values):
             lanes = slice(c * BLK, (c + 1) * BLK)
-            mine[d, :, lanes] = (value + xin[d, :, lanes].astype(F32)).astype(BF16)
-        if d:
-            for i in range(2):
-                at = pl.ds(i * half, half)
-                a_copies[d, i] = remote(mine.at[d, at], ain.at[d, at], as_.at[d, i], ar.at[d, i], a_peer[d])
-            a_copies[d, 0].start()
-    for d in range(1, QA):
-        a_copies[d, 1].start()
+            mine[p, :, lanes] = (value + xin[p, :, lanes].astype(F32)).astype(BF16)
+        for d in (2, 3, 1):
+            at = pl.ds(d * quarter, quarter)
+            a_copies[d, p] = remote(mine.at[p, at], ain.at[p, at], as_.at[d, p], ar.at[d, p], a_peer[d])
+            a_copies[d, p].start()
+
+    b_copies = {}
+
+    def phase(p):
+        total = mine[p, 0:quarter].astype(F32)
+        for d in range(1, QA):
+            a_copies[d, p].wait_recv()
+        for d in range(1, QA):
+            total = total + ain[p, d * quarter:(d + 1) * quarter].astype(F32)
+        summed[p * quarter:(p + 1) * quarter] = total.astype(BF16)
+        for spot in range(2 * p, 2 * p + 2):
+            d = SPOTS[spot]
+            if d:
+                if d not in NEAR:
+                    pl.semaphore_wait(relay.at[(3, 5, 4).index(d)], 1)
+                rows = pl.ds(spot * ROWS, ROWS)
+                b_copies[d] = remote(summed.at[rows], bin_.at[d], bs.at[d], br.at[d], b_peer[d])
+                b_copies[d].start()
+
+    phase(0)
+    for copy in wy_copies:
+        copy.wait_recv()
+    ref = w_all.at[pl.ds(core * (2 * NY) + xh * NY, NY)]
+    wx_copy = remote(ref, ref, wxs.at[0], wxr.at[0], at_hid(1 - xh, y, core))
+    wx_copy.start()
+    for p in range(1, PHASES):
+        phase(p)
 
     r = lax.broadcasted_iota(jnp.int32, (share, BLK), 0)
     lane = lax.broadcasted_iota(jnp.int32, (share, BLK), 1)
     spare = jnp.zeros((share, BLK - share), F32)
     row = jnp.concatenate([jnp.broadcast_to(bias[...], (share, share)), spare], axis=1)
     rest = jnp.sum(jnp.where(r == lane, row, 0.0), axis=1, keepdims=True)
-    channels = NH * PART
+    channels = NG * PART
     we_wide = jnp.concatenate([we_own[...].astype(F32), jnp.zeros((share, BLK - channels), F32)], axis=1)
     for i in range(3):
         digit = rest.astype(BF16).astype(F32)
         we_wide = jnp.where(lane == channels + i, digit, we_wide)
         rest = rest - digit
     we_all[h] = we_wide.astype(BF16)
-
-    for copy in wy_copies:
-        copy.wait_recv()
-    ref = w_all.at[pl.ds(core * (2 * NY) + xh * NY, NY)]
-    wx_copy = remote(ref, ref, wxs.at[0], wxr.at[0], at_hid(1 - xh, y, core))
-    wx_copy.start()
 
     small = []
     for d in range(1, NH):
@@ -205,21 +228,6 @@
             for copy in small[d - 1]:
                 copy.start()
 
-    b_copies = {}
-    for i in range(2):
-        for d in range(1, QA):
-            a_copies[d, i].wait_recv()
-        at = pl.ds(i * half, half)
-        total = mine[0, at].astype(F32)
-        for d in range(1, QA):
-            total = total + ain[d, at].astype(F32)
-        summed[at] = total.astype(BF16)
-        for spot in range(i * KB // 2, (i + 1) * KB // 2):
-            d = SPOTS[spot]
-            if d:
-                rows = pl.ds(spot * ROWS, ROWS)
-                b_copies[d] = remote(summed.at[rows], bin_.at[d], bs.at[d], br.at[d], b_peer[d])
-                b_copies[d].start()
     my_lanes = pl.ds(pl.multiple_of(tile_of(h) * BLK, BLK), BLK)
     wx_copy.wait_recv()
     ref = w_all.at[pl.ds(core * (2 * NY), 2 * NY)]
@@ -240,19 +248,20 @@
     wc_copy.wait_recv()
     down_t[...] = w_all[:, 2].reshape(NH * share, wide).T
     total = summed[pl.ds((KB - 1) * ROWS, ROWS)].astype(F32)
-    for d in (1, 7, 2, 6, 3, 5, 4):
+    for d in SPOTS[:-1]:
         b_copies[d].wait_recv()
         total = total + bin_[d].astype(F32)
-    for i in range(TILES):
-        for c in range(3):
-            tiles_out[i, c:c + 1] = total[i:i + 1, c * BLK:(c + 1) * BLK]
-        r, c = (10 + i, 0) if i < 6 else (4 + i, 1)
-        tiles_out[i, 3:4] = total[r:r + 1, c * BLK:(c + 1) * BLK]
-        tiles_out[i, 4:8] = jnp.broadcast_to(total[10:11, 2 * BLK + i:2 * BLK + i + 1], (4, BLK))
+    tiles_out[...] = jnp.zeros(tiles_out.shape, F32)
+    for i in range(HALF):
+        for c in range(PART + 1):
+            r = HALF * (c % 3) + i
+            tiles_out[i, c:c + 1] = total[r:r + 1, (c // 3) * BLK:(c // 3 + 1) * BLK]
     t_copies = []
-    for d in range(1, NH):
-        to = h_index[d]
-        t_copies.append(remote(tiles_out.at[tile_of(to)], tiles_in.at[h], ts.at[d], tr.at[d], h_peer[d]))
+    t_index = [xh * NG + lax.rem(group + d, NG) for d in range(NG)]
+    for d in range(1, NG):
+        to = t_index[d]
+        src = tiles_out.at[tile_of(to) - xh * HALF]
+        t_copies.append(remote(src, tiles_in.at[group], ts.at[d], tr.at[d], (lon, to)))
 
         @pl.when(active(to))
         def _():
@@ -266,17 +275,17 @@
 
     @pl.when(active(h))
     def _():
-        tiles_in[h] = tiles_out[tile_of(h)]
+        tiles_in[group] = tiles_out[tile_of(h) - xh * HALF]
         for copy in t_copies:
             copy.wait_recv()
         sums = tiles_in[...]
-        number = sums[0, 4:5]
+        number = sums[0, PART:PART + 1]
         sums = sums[:, 0:PART].reshape(channels, BLK)
         extra = jnp.where(lax.broadcasted_iota(jnp.int32, (BLK - channels, BLK), 0) < 3, number, 0.0)
         sums = jnp.concatenate([sums, extra], axis=0)
         we = we_all[...].reshape(NH * share, BLK)
         smooth = jnp.zeros((NH * share, BLK), F32)
-        for _ in range(3):
+        for _ in range(2):
             digit = sums.astype(BF16)
             smooth = smooth + jnp.dot(we, digit, preferred_element_type=F32)
             sums = sums - digit.astype(F32)
@@ -312,6 +321,10 @@
         def _():
             for copy in small[d - 1]:
                 copy.wait_send()
+    for d in range(1, NG):
+
+        @pl.when(active(t_index[d]))
+        def _():
             t_copies[d - 1].wait_send()
 
     @pl.when(active(h))
@@ -338,26 +351,26 @@
             pltpu.VMEM((1, blocks), jnp.int32),
             pltpu.VMEM((1, share), F32),
             pltpu.VMEM((1, lat), F32),
-            pltpu.VMEM((share, NH * PART), BF16),
+            pltpu.VMEM((share, NG * PART), BF16),
             pltpu.VMEM((16, rows), BF16),
             pltpu.VMEM((blocks * 16, BLK), F32),
             pltpu.VMEM((blocks, (PART + 1) * BLK), BF16),
-            pltpu.VMEM((QA, PIECE, WIDE), BF16),
-            pltpu.VMEM((QA, PIECE, WIDE), BF16),
-            pltpu.VMEM((QA, PIECE, WIDE), BF16),
-            pltpu.VMEM((QA, PIECE, WIDE), BF16),
+            pltpu.VMEM((PHASES, PIECE, WIDE), BF16),
+            pltpu.VMEM((PHASES, PIECE, WIDE), BF16),
+            pltpu.VMEM((PHASES, PIECE, WIDE), BF16),
+            pltpu.VMEM((PHASES, PIECE, WIDE), BF16),
             pltpu.VMEM((PIECE, WIDE), BF16),
             pltpu.VMEM((KB, ROWS, WIDE), BF16),
-            pltpu.VMEM((TILES, 8, BLK), F32),
-            pltpu.VMEM((NH, 8, BLK), F32),
+            pltpu.VMEM((HALF, 16, BLK), F32),
+            pltpu.VMEM((NG, 16, BLK), F32),
             pltpu.VMEM((NH, 3, share, lat), BF16),
             pltpu.VMEM((lat, NH * share), BF16),
             pltpu.VMEM((NH, share, BLK), BF16),
             pltpu.VMEM((NH, share, BLK), BF16),
             pltpu.VMEM((lat, BLK), F32),
             pltpu.VMEM((lat, BLK), BF16),
-            dma, dma((8,)),
-            dma((QA,)), dma((QA,)), dma((QA, 2)), dma((QA, 2)), dma((KB,)), dma((KB,)),
+            pltpu.SemaphoreType.REGULAR((3,)), dma, dma((8,)),
+            dma((QA,)), dma((QA,)), dma((QA, PHASES)), dma((QA, PHASES)), dma((KB,)), dma((KB,)),
             dma((NY,)), dma((NY,)), dma((2,)), dma((2,)),
             dma((NH,)), dma((NH,)), dma((NH,)), dma((NH,)), dma((NH,)), dma((NH,)), dma((NH,)), dma((NH,)),
         ],

time: 68.9 us -> 67 us (0.972)
  Pallas kernels: 67.2 us -> 65.3 us
    pallas_call x1, Pallas kernels: 67.2 us -> 65.3 us  [local(): pl.pallas_call(functools.partial(kernel, math.sqrt(TILES / blocks)), out_...]
where the time goes in v4:
time: 67 us; the launch traced here: 66.8 us
  Pallas kernels  65.3 us (97%)
  local copies, waits for them, and re-layouts  1.53 us (2%)
    pallas_call x1, Pallas kernels, local(): pl.pallas_call(functools.partial(kernel, math.sqrt(TILES / blocks)), out_...  65.3 us
    unnamed x1, local copies, waits for them, and re-layouts  1.53 us

profile of v4, /device:TPU:1, one launch (start us, length us, event | category | flops | bytes accessed | tf_op | source)
XLA Modules:
  0.0 66.8 jit_solution(6041127024346098926)
XLA Ops:
  0.0 65.3 %shard_map.100 = bf16[32,1280]{1,0:T(8,128)(2,1)} custom-call(bf16[64,32768]{1,0:T(8,128)(2,1)} %bitcast.10, s32[1,256]{1,0:T(1,128)} %bitcast.17, s32[1,256]{1,0:T(1,128)} %bitcast.18, bf16[32,64]{1,0:T(8,128)(2,1)} %bitcast.15, f32[1,32]{1,0:T(1,128)} %bitcast.19, bf16[32,1280]{1,0:T(8,128)(2,1)} %bitcast.12, f32[1,512]{1,0:T(1,128)} %bitcast.16, ...), custom_call_target="tpu_custom_call" | custom-call | tf_op jit(solution)/shard_map/pallas_call | solution.py:344
  65.3 1.5 %copy.12 = bf16[1280,32]{0,1:T(8,128)(2,1)} copy(bf16[1280,32]{0,1:T(8,128)(2,1)} %bitcast.11) | data formatting | bytes 163840

commit v5 on v4

--- a/solution.py
+++ b/solution.py
@@ -25,7 +25,7 @@
 WIDE = 3 * BLK
 PIECE = KB * ROWS
 PHASES = KB // 2
-SPOTS = (2, 6, 1, 7, 3, 5, 4, 0)
+SPOTS = (4, 3, 5, 2, 6, 1, 7, 0)
 NEAR = (1, 7, 2, 6)
 F32 = jnp.float32
 BF16 = jnp.bfloat16

time: 67 us -> 64.3 us (0.960)
  Pallas kernels: 65.3 us -> 62.2 us
    pallas_call x1, Pallas kernels: 65.3 us -> 62.2 us  [local(): pl.pallas_call(functools.partial(kernel, math.sqrt(TILES / blocks)), out_...]
where the time goes in v5:
time: 64.3 us; the launch traced here: 63.7 us
  Pallas kernels  62.2 us (97%)
  local copies, waits for them, and re-layouts  1.53 us (2%)
    pallas_call x1, Pallas kernels, local(): pl.pallas_call(functools.partial(kernel, math.sqrt(TILES / blocks)), out_...  62.2 us
    unnamed x1, local copies, waits for them, and re-layouts  1.53 us

profile of v5, /device:TPU:1, one launch (start us, length us, event | category | flops | bytes accessed | tf_op | source)
XLA Modules:
  0.0 63.7 jit_solution(7397947056241608630)
XLA Ops:
  0.0 62.2 %shard_map.100 = bf16[32,1280]{1,0:T(8,128)(2,1)} custom-call(bf16[64,32768]{1,0:T(8,128)(2,1)} %bitcast.10, s32[1,256]{1,0:T(1,128)} %bitcast.17, s32[1,256]{1,0:T(1,128)} %bitcast.18, bf16[32,64]{1,0:T(8,128)(2,1)} %bitcast.15, f32[1,32]{1,0:T(1,128)} %bitcast.19, bf16[32,1280]{1,0:T(8,128)(2,1)} %bitcast.12, f32[1,512]{1,0:T(1,128)} %bitcast.16, ...), custom_call_target="tpu_custom_call" | custom-call | tf_op jit(solution)/shard_map/pallas_call | solution.py:344
  62.2 1.5 %copy.12 = bf16[1280,32]{0,1:T(8,128)(2,1)} copy(bf16[1280,32]{0,1:T(8,128)(2,1)} %bitcast.11) | data formatting | bytes 163840

commit v6 on v5

--- a/solution.py
+++ b/solution.py
@@ -47,13 +47,11 @@
     core = lax.rem(h, 2)
     y = lax.rem(h // 2, NY)
     xh = h // (2 * NY)
-    off = 2 * core
-    v = lax.rem(z + off, NZ)
-    g = v // QA
-    q = lax.rem(v, QA)
+    g = z // QA
+    q = lax.rem(z, QA)
 
     def at_v(value):
-        return (x * NZ + lax.rem(value - off + NZ, NZ), h)
+        return (x * NZ + value, h)
 
     def at_hid(xh, y, core):
         return (lon, (xh * NY + y) * 2 + core)
@@ -100,7 +98,7 @@
         o = owner[...]
         o = jnp.where(t < 0, (o + LON - 1) & (LON - 1), jnp.where(t >= TILES, (o + 1) & (LON - 1), o))
         t = jnp.where(t < 0, TILES - 1, jnp.where(t >= TILES, 0, t))
-        u = ((o & (NZ - 1)) + off) & (NZ - 1)
+        u = o & (NZ - 1)
         side = (o >> 5) ^ x
         dq = ((u & (QA - 1)) - q) & (QA - 1)
         dk = ((u >> 2) - g) & (KB - 1)

time: 64.3 us -> 64 us (level)
  no operation moved by 1% of the time
where the time goes in v6:
time: 64 us; the launch traced here: 63.4 us
  Pallas kernels  61.9 us (97%)
  local copies, waits for them, and re-layouts  1.53 us (2%)
    pallas_call x1, Pallas kernels, local(): pl.pallas_call(functools.partial(kernel, math.sqrt(TILES / blocks)), out_...  61.9 us
    unnamed x1, local copies, waits for them, and re-layouts  1.53 us

profile of v6, /device:TPU:1, one launch (start us, length us, event | category | flops | bytes accessed | tf_op | source)
XLA Modules:
  0.0 63.4 jit_solution(15051742562541528114)
XLA Ops:
  0.0 61.9 %shard_map.100 = bf16[32,1280]{1,0:T(8,128)(2,1)} custom-call(bf16[64,32768]{1,0:T(8,128)(2,1)} %bitcast.10, s32[1,256]{1,0:T(1,128)} %bitcast.17, s32[1,256]{1,0:T(1,128)} %bitcast.18, bf16[32,64]{1,0:T(8,128)(2,1)} %bitcast.15, f32[1,32]{1,0:T(1,128)} %bitcast.19, bf16[32,1280]{1,0:T(8,128)(2,1)} %bitcast.12, f32[1,512]{1,0:T(1,128)} %bitcast.16, ...), custom_call_target="tpu_custom_call" | custom-call | tf_op jit(solution)/shard_map/pallas_call | solution.py:342
  61.9 1.5 %copy.12 = bf16[1280,32]{0,1:T(8,128)(2,1)} copy(bf16[1280,32]{0,1:T(8,128)(2,1)} %bitcast.11) | data formatting | bytes 163840
